TPU v7x, 256 devices: a whole 4x4x8 slice. The times are simulated.
256 devices in a mesh: seq: 32 (over y, z_hi, core), head: 8 (over x, z_lo).
Axes of the slice: x: 4, y: 4, z: 8 (z_hi: 4, z_lo: 2; z = z_hi * 2 + z_lo), core: 2. Of those that a mesh axis runs over, the one named last changes fastest.
Arguments:
- prompt_q: bfloat16 [512, 5120], P(('seq', 'head')), may hold values from -8 to 8
- prompt_k: bfloat16 [512, 1024], P(('seq', 'head')), may hold values from -8 to 8
- prompt_v: bfloat16 [512, 1024], P(('seq', 'head')), may hold values from -6 to 6
- prompt_grad: bfloat16 [512, 5120], P(('seq', 'head')), may hold values from -6 to 6
- segment_ids: int32 [512], replicated, may hold values from 0 to 127, never falling along the last dimension, each value on 1 to 24 neighbouring positions
- answer_q: bfloat16 [32, 256, 5120], P('seq', None, 'head'), may hold values from -8 to 8
- answer_k: bfloat16 [32, 256, 1024], P('seq', None, 'head'), may hold values from -8 to 8
- answer_v: bfloat16 [32, 256, 1024], P('seq', None, 'head'), may hold values from -6 to 6
- answer_grad: bfloat16 [32, 256, 5120], P('seq', None, 'head'), may hold values from -6 to 6
- answer_lengths: int32 [32], P('seq'), may hold values from 1 to 256, 5120 in all
Outputs:
- prompt_out: bfloat16 [512, 5120], P(('seq', 'head'))
- prompt_dq: bfloat16 [512, 5120], P(('seq', 'head'))
- prompt_dk: bfloat16 [512, 1024], P(('seq', 'head'))
- prompt_dv: bfloat16 [512, 1024], P(('seq', 'head'))
- answer_out: bfloat16 [32, 256, 5120], P('seq', None, 'head')
- answer_dq: bfloat16 [32, 256, 5120], P('seq', None, 'head')
- answer_dk: bfloat16 [32, 256, 1024], P('seq', None, 'head')
- answer_dv: bfloat16 [32, 256, 1024], P('seq', None, 'head')
Inputs may be any that keep to these rules, and one draw needn't show every extreme that they name: `segment_ids`: never falls along the prompt; each timestamp segment spans 1 to 24 positions, one exactly 24. `answer_lengths`: one answer has exactly 256 tokens.
All inputs are finite; a program needn't handle non-finite values. No bound on the sum of `answer_lengths` on one device may be relied on, other than what follows from the above.
Results may differ from a plain program's by a relative error of at most 0.038.
Values may be sent and summed in bfloat16 or wider, within the bound.
No kernel may reach another device: no remote copies, remote signals or barrier semaphores. Data moves between devices by JAX's collectives and lax.ppermute only.
A program may use at most 64 MiB of HBM per device.

v0:
```python
import math

import jax
import jax.numpy as jnp
from jax import lax
from jax.sharding import PartitionSpec as P

HEADS = 40
KV_HEADS = 8
HEAD_DIM = 128


def score_block(queries, keys_block, scaling):
    return (
        jnp.einsum("rgnd,cgd->gnrc", queries, keys_block, preferred_element_type=jnp.float32)
        * scaling
    )


def add_stats(running, masked):
    running_max, running_sum = running
    new_max = jnp.maximum(running_max, jnp.max(masked, axis=-1))
    new_sum = running_sum * jnp.exp(running_max - new_max) + jnp.sum(
        jnp.exp(masked - new_max[..., None]), axis=-1
    )
    return (new_max, new_sum)


def weights_of(masked, log_total):
    weights = jnp.exp(masked - log_total[..., None])
    return (weights, weights.astype(jnp.bfloat16))


def block_grads(
    queries, out_grads, keys_block, values_block, masked, log_total, row_delta, scaling
):
    weights, weights_low = weights_of(masked, log_total)
    value_grad = jnp.einsum(
        "gnrc,rgnd->cgd", weights_low, out_grads, preferred_element_type=jnp.float32
    )
    prob_grad = jnp.einsum(
        "rgnd,cgd->gnrc", out_grads, values_block, preferred_element_type=jnp.float32
    )
    score_grad = (weights * (prob_grad - row_delta[..., None]) * scaling).astype(jnp.bfloat16)
    query_grad = jnp.einsum(
        "gnrc,cgd->rgnd", score_grad, keys_block, preferred_element_type=jnp.float32
    )
    key_grad = jnp.einsum("gnrc,rgnd->cgd", score_grad, queries, preferred_element_type=jnp.float32)
    return (query_grad, key_grad, value_grad)


def keep_same(current):
    return current


def body(
    prompt_q,
    prompt_k,
    prompt_v,
    prompt_grad,
    segment_ids,
    answer_q,
    answer_k,
    answer_v,
    answer_grad,
    answer_lengths,
):
    head_count = lax.axis_size("head")
    local_groups = KV_HEADS // head_count
    group_size = HEADS // KV_HEADS
    group_width = local_groups * HEAD_DIM
    scaling = 1.0 / math.sqrt(HEAD_DIM)
    query_shape = (local_groups, group_size, HEAD_DIM)
    key_shape = (local_groups, HEAD_DIM)
    arrived = (
        lax.all_to_all(prompt_q, "head", split_axis=1, concat_axis=0, tiled=True),
        lax.all_to_all(prompt_grad, "head", split_axis=1, concat_axis=0, tiled=True),
        lax.all_to_all(prompt_k, "head", split_axis=1, concat_axis=0, tiled=True),
        lax.all_to_all(prompt_v, "head", split_axis=1, concat_axis=0, tiled=True),
    )
    prompt_count = arrived[0].shape[0]
    prompt_queries = arrived[0].reshape((prompt_count,) + query_shape)
    prompt_grads = arrived[1].reshape((prompt_count,) + query_shape)
    answer_count = answer_q.shape[1]
    answer_queries = answer_q[0].reshape((answer_count,) + query_shape)
    answer_keys = answer_k[0].reshape((answer_count,) + key_shape)
    answer_values = answer_v[0].reshape((answer_count,) + key_shape)
    positions = jnp.arange(answer_count, dtype=jnp.int32)
    length = answer_lengths[0]
    live_rows = positions < length
    answer_grads = answer_grad[0].reshape((answer_count,) + query_shape)
    answer_grads = jnp.where(
        live_rows[:, None, None, None], answer_grads, jnp.zeros_like(answer_grads)
    )
    my_segments = lax.dynamic_slice_in_dim(
        segment_ids, lax.axis_index("seq") * prompt_count, prompt_count
    )
    top_segment = my_segments[-1]
    full_rows, full_values = (
        lax.all_gather(prompt_k, ("seq", "head"), axis=0, tiled=True),
        lax.all_gather(prompt_v, ("seq", "head"), axis=0, tiled=True),
    )
    column = lax.axis_index("head") * group_width
    all_keys = lax.dynamic_slice_in_dim(full_rows, column, group_width, 1)
    all_values = lax.dynamic_slice_in_dim(full_values, column, group_width, 1)
    prompt_total = all_keys.shape[0]
    block_len = min(256, prompt_total)
    block_count = prompt_total // block_len
    segment_blocks = segment_ids.reshape(block_count, block_len)
    key_blocks = (
        all_keys.reshape((block_count, block_len) + key_shape),
        all_values.reshape((block_count, block_len) + key_shape),
        segment_blocks,
    )

    def prompt_masked(keys_block, segments_block):
        visible = segments_block[None, :] <= my_segments[:, None]
        return jnp.where(
            visible[None, None], score_block(prompt_queries, keys_block, scaling), -jnp.inf
        )

    tile_len = min(256, answer_count)
    tile_count = answer_count // tile_len
    tile_ids = jnp.arange(tile_count, dtype=jnp.int32)
    tile_offsets = jnp.arange(tile_len, dtype=jnp.int32)
    query_tiles = answer_queries.reshape((tile_count, tile_len) + query_shape)
    grad_tiles = answer_grads.reshape((tile_count, tile_len) + query_shape)
    key_tiles = answer_keys.reshape((tile_count, tile_len) + key_shape)
    value_tiles = answer_values.reshape((tile_count, tile_len) + key_shape)

    def self_masked(query_tile, key_tile, query_id, key_id):
        query_pos = query_id * tile_len + tile_offsets
        key_pos = key_id * tile_len + tile_offsets
        visible = (key_pos[None, :] <= query_pos[:, None]) & (key_pos[None, :] < length)
        return jnp.where(visible[None, None], score_block(query_tile, key_tile, scaling), -jnp.inf)

    def by_tile(stat):
        return jnp.moveaxis(stat.reshape(local_groups, group_size, tile_count, tile_len), 2, 0)

    prompt_shape = (local_groups, group_size, prompt_count)
    answer_shape = (local_groups, group_size, answer_count)
    start_prompt = (
        jnp.full(prompt_shape, -jnp.inf, jnp.float32),
        jnp.zeros(prompt_shape, jnp.float32),
    )
    start_answer = (
        jnp.full(answer_shape, -jnp.inf, jnp.float32),
        jnp.zeros(answer_shape, jnp.float32),
    )

    def first_pass(running, block_data):
        keys_block, values_block, segments_block = block_data
        prompt_stats, answer_stats = running

        def first_visit_block(current):
            return add_stats(current, prompt_masked(keys_block, segments_block))

        prompt_stats = lax.cond(
            segments_block[0] <= top_segment, first_visit_block, keep_same, prompt_stats
        )
        answer_stats = add_stats(answer_stats, score_block(answer_queries, keys_block, scaling))
        return ((prompt_stats, answer_stats), None)

    (prompt_stats, answer_stats), unused = lax.scan(
        first_pass, (start_prompt, start_answer), key_blocks
    )
    prompt_log = prompt_stats[0] + jnp.log(prompt_stats[1])

    def self_stats(unused_carry, packed):
        query_id, query_tile, tile_max, tile_sum = packed

        def over_keys(current, key_packed):
            key_id, key_tile = key_packed

            def visit_tile(stat_pair):
                return add_stats(stat_pair, self_masked(query_tile, key_tile, query_id, key_id))

            return (lax.cond(key_id <= query_id, visit_tile, keep_same, current), None)

        result, unused_keys = lax.scan(over_keys, (tile_max, tile_sum), (tile_ids, key_tiles))
        return (None, result)

    unused, (tiles_max, tiles_sum) = lax.scan(
        self_stats,
        None,
        (tile_ids, query_tiles, by_tile(answer_stats[0]), by_tile(answer_stats[1])),
    )
    log_tiles = tiles_max + jnp.log(tiles_sum)
    answer_log = jnp.moveaxis(log_tiles, 0, 2).reshape(local_groups, group_size, answer_count)

    def self_output(unused_carry, packed):
        query_id, query_tile, log_tile = packed
        zero_acc = jnp.zeros((tile_len,) + query_shape, jnp.float32)

        def over_keys(current, key_packed):
            key_id, key_tile, value_tile = key_packed

            def visit_tile(running):
                weights, weights_low = weights_of(
                    self_masked(query_tile, key_tile, query_id, key_id), log_tile
                )
                return running + jnp.einsum(
                    "gnrc,cgd->rgnd", weights_low, value_tile, preferred_element_type=jnp.float32
                )

            return (lax.cond(key_id <= query_id, visit_tile, keep_same, current), None)

        result, unused_keys = lax.scan(over_keys, zero_acc, (tile_ids, key_tiles, value_tiles))
        return (None, result)

    unused, self_out = lax.scan(self_output, None, (tile_ids, query_tiles, log_tiles))
    answer_start = self_out.reshape((answer_count,) + query_shape)
    prompt_start = jnp.zeros((prompt_count,) + query_shape, jnp.float32)

    def second_pass(running, block_data):
        keys_block, values_block, segments_block = block_data
        prompt_acc, answer_acc = running

        def second_visit_block(current):
            weights, weights_low = weights_of(prompt_masked(keys_block, segments_block), prompt_log)
            return current + jnp.einsum(
                "gnrc,cgd->rgnd", weights_low, values_block, preferred_element_type=jnp.float32
            )

        prompt_acc = lax.cond(
            segments_block[0] <= top_segment, second_visit_block, keep_same, prompt_acc
        )
        weights, weights_low = weights_of(
            score_block(answer_queries, keys_block, scaling), answer_log
        )
        answer_acc = answer_acc + jnp.einsum(
            "gnrc,cgd->rgnd", weights_low, values_block, preferred_element_type=jnp.float32
        )
        return ((prompt_acc, answer_acc), None)

    (prompt_acc, answer_acc), unused = lax.scan(
        second_pass, (prompt_start, answer_start), key_blocks
    )
    prompt_out = prompt_acc.astype(jnp.bfloat16)
    answer_out = jnp.where(
        live_rows[:, None, None, None], answer_acc, jnp.zeros_like(answer_acc)
    ).astype(jnp.bfloat16)
    prompt_delta = jnp.einsum(
        "rgnd,rgnd->gnr", prompt_out, prompt_grads, preferred_element_type=jnp.float32
    )
    answer_delta = jnp.einsum(
        "rgnd,rgnd->gnr", answer_out, answer_grads, preferred_element_type=jnp.float32
    )
    delta_tiles = by_tile(answer_delta)
    zero_tiles = jnp.zeros((tile_count, tile_len) + key_shape, jnp.float32)

    def self_grads(running, packed):
        key_acc, value_acc = running
        query_id, query_tile, grad_tile, log_tile, delta_tile = packed
        zero_acc = jnp.zeros((tile_len,) + query_shape, jnp.float32)

        def over_keys(current, key_packed):
            key_id, key_tile, value_tile = key_packed

            def visit_tile(current_state):
                query_acc, keys_sum, values_sum = current_state
                part_q, part_k, part_v = block_grads(
                    query_tile,
                    grad_tile,
                    key_tile,
                    value_tile,
                    self_masked(query_tile, key_tile, query_id, key_id),
                    log_tile,
                    delta_tile,
                    scaling,
                )
                keys_sum = lax.dynamic_update_index_in_dim(
                    keys_sum,
                    lax.dynamic_index_in_dim(keys_sum, key_id, 0, False) + part_k,
                    key_id,
                    0,
                )
                values_sum = lax.dynamic_update_index_in_dim(
                    values_sum,
                    lax.dynamic_index_in_dim(values_sum, key_id, 0, False) + part_v,
                    key_id,
                    0,
                )
                return (query_acc + part_q, keys_sum, values_sum)

            return (lax.cond(key_id <= query_id, visit_tile, keep_same, current), None)

        (query_acc, key_acc, value_acc), unused_keys = lax.scan(
            over_keys, (zero_acc, key_acc, value_acc), (tile_ids, key_tiles, value_tiles)
        )
        return ((key_acc, value_acc), query_acc)

    (self_key_grad, self_value_grad), self_query_grad = lax.scan(
        self_grads,
        (zero_tiles, zero_tiles),
        (tile_ids, query_tiles, grad_tiles, log_tiles, delta_tiles),
    )
    zero_keys = jnp.zeros((block_len,) + key_shape, jnp.float32)

    def grad_pass(running, block_data):
        keys_block, values_block, segments_block = block_data
        prompt_qgrad, answer_qgrad = running

        def grad_visit_block(current):
            part_q, part_k, part_v = block_grads(
                prompt_queries,
                prompt_grads,
                keys_block,
                values_block,
                prompt_masked(keys_block, segments_block),
                prompt_log,
                prompt_delta,
                scaling,
            )
            return (current + part_q, part_k, part_v)

        def pass_over(current):
            return (current, zero_keys, zero_keys)

        prompt_qgrad, prompt_kterm, prompt_vterm = lax.cond(
            segments_block[0] <= top_segment, grad_visit_block, pass_over, prompt_qgrad
        )
        part_q, part_k, part_v = block_grads(
            answer_queries,
            answer_grads,
            keys_block,
            values_block,
            score_block(answer_queries, keys_block, scaling),
            answer_log,
            answer_delta,
            scaling,
        )
        return (
            (prompt_qgrad, answer_qgrad + part_q),
            (prompt_kterm + part_k, prompt_vterm + part_v),
        )

    answer_qstart = self_query_grad.reshape((answer_count,) + query_shape)
    (prompt_qgrad, answer_qgrad), (key_terms, value_terms) = lax.scan(
        grad_pass, (prompt_start, answer_qstart), key_blocks
    )
    key_sums, value_sums = (
        lax.psum_scatter(
            key_terms.reshape(prompt_total, group_width), "seq", scatter_dimension=0, tiled=True
        ),
        lax.psum_scatter(
            value_terms.reshape(prompt_total, group_width), "seq", scatter_dimension=0, tiled=True
        ),
    )
    returned = (
        lax.all_to_all(
            prompt_out.reshape(prompt_count, -1), "head", split_axis=0, concat_axis=1, tiled=True
        ),
        lax.all_to_all(
            prompt_qgrad.astype(jnp.bfloat16).reshape(prompt_count, -1),
            "head",
            split_axis=0,
            concat_axis=1,
            tiled=True,
        ),
        lax.all_to_all(
            key_sums.astype(jnp.bfloat16), "head", split_axis=0, concat_axis=1, tiled=True
        ),
        lax.all_to_all(
            value_sums.astype(jnp.bfloat16), "head", split_axis=0, concat_axis=1, tiled=True
        ),
    )
    answer_dq = answer_qgrad.astype(jnp.bfloat16).reshape(1, answer_count, -1)
    answer_dk = self_key_grad.astype(jnp.bfloat16).reshape(1, answer_count, group_width)
    answer_dv = self_value_grad.astype(jnp.bfloat16).reshape(1, answer_count, group_width)
    return (
        returned[0],
        returned[1],
        returned[2],
        returned[3],
        answer_out.reshape(1, answer_count, -1),
        answer_dq,
        answer_dk,
        answer_dv,
    )


def solution(mesh):
    return jax.shard_map(
        body,
        mesh=mesh,
        in_specs=(
            P(("seq", "head"), None),
            P(("seq", "head"), None),
            P(("seq", "head"), None),
            P(("seq", "head"), None),
            P(),
            P("seq", None, "head"),
            P("seq", None, "head"),
            P("seq", None, "head"),
            P("seq", None, "head"),
            P("seq"),
        ),
        out_specs=(
            P(("seq", "head"), None),
            P(("seq", "head"), None),
            P(("seq", "head"), None),
            P(("seq", "head"), None),
            P("seq", None, "head"),
            P("seq", None, "head"),
            P("seq", None, "head"),
            P("seq", None, "head"),
        ),
        check_vma=False,
    )
```

profile of v0, /device:TPU:1, one launch (start us, length us, event | category | flops | bytes accessed | tf_op | source)
XLA Modules:
  0.0 1308.0 jit_solution(3781593049533824012)
XLA Ops:
  8.7 6.2 all-to-all-start.2
  20.0 4.3 all-to-all-start
  26.2 3.1 all-to-all-done
  30.0 513.5 %all-gather.5.cloned.1.call-done = bf16[256,2,1024]{2,1,0:T(2,128)(2,1)} async-done(((bf16[1,2,1024]{2,1,0:T(2,128)(2,1)}), bf16[256,2,1024]{2,1,0:T(2,128)(2,1)}) %all-gather.5.cloned.1.call-update) | async-done | bytes 1048592 | tf_op jit(solution)/shard_map/all_gather | solution.py:100
  543.5 2.2 reshape.596
  546.6 524.2 %all-gather.7.cloned.1.call-done = bf16[256,2,1024]{2,1,0:T(2,128)(2,1)} async-done(((bf16[1,2,1024]{2,1,0:T(2,128)(2,1)}), bf16[256,2,1024]{2,1,0:T(2,128)(2,1)}) %all-gather.7.cloned.1.call-update) | async-done | bytes 1048592 | tf_op jit(solution)/shard_map/all_gather | solution.py:101
  1070.8 2.3 reshape.598
  1074.0 5.5 while.59
  1081.6 1.3 copy.80
  1083.0 5.3 while.57
  1092.2 1.3 copy.91
  1095.5 16.8 %while.58 = (s32[]{:T(128)}, f32[16,1,5,128]{3,0,2,1:T(8,128)}, f32[256,1,5,128]{0,3,2,1:T(8,128)S(1)}, f32[2,256,1,128]{3,1,2,0:T(8,128)}, f32[2,256,1,128]{3,1...) while((s32[]{:T(128)}, f32[16,1,5,128]{3,0,2,1:T(8,128)}, ...), condition=%wide.region_17.18_spmd, body=%wide.region_14.17_spmd.sunk | while | flops 448346112 | bytes 16024427 | solution.py:339
  1097.6 5.2 conditional.8
  1099.4 1.5 fusion.45
  1114.4 3.3 all-to-all-start.3
  1119.1 3.6 all-to-all-done.3
  1122.7 3.3 all-to-all-start.1
  1126.1 73.4 %reduce-scatter.3.cloned.1.call-done = f32[16,128]{1,0:T(8,128)} async-done(((f32[512,128]{1,0:T(8,128)}), f32[16,128]{1,0:T(8,128)}) %reduce-scatter.3.cloned.1.call-update) | async-done | bytes 8208 | tf_op jit(solution)/shard_map/reduce_scatter | solution.py:343
  1199.5 1.3 convert_element_type.110
  1200.8 4.1 all-to-all-start.4
  1205.9 82.9 %reduce-scatter.5.cloned.1.call-done = f32[16,128]{1,0:T(8,128)} async-done(((f32[512,128]{1,0:T(8,128)}), f32[16,128]{1,0:T(8,128)}) %reduce-scatter.5.cloned.1.call-update) | async-done | bytes 8208 | tf_op jit(solution)/shard_map/reduce_scatter | solution.py:346
  1288.8 1.3 convert_element_type.111
  1290.1 4.1 all-to-all-start.5
  1297.7 1.4 all-to-all-done.5
  (202 shorter events, 46.9 us)
Async XLA Ops:
  7.2 10.8 copy-start
  7.2 536.3 %all-gather.5.cloned.1.call-start = ((), (), s32[]{:S(2)}) async-start(), calls=%async_computation.10 | async-start | bytes 1052672 | tf_op jit(solution)/shard_map/all_gather | solution.py:100
  7.9 1062.9 %all-gather.7.cloned.1.call-start = ((), (), s32[]{:S(2)}) async-start(), calls=%async_computation.11 | async-start | bytes 1052672 | tf_op jit(solution)/shard_map/all_gather | solution.py:101
  8.7 11.3 all-to-all-start.2
  17.8 7.3 copy-start.3
  17.9 6.5 copy-start.24
  18.0 6.4 copy-start.26
  20.0 9.4 all-to-all-start
  24.2 1175.3 %reduce-scatter.3.cloned.1.call-start = ((), (), s32[]{:S(2)}) async-start(), calls=%async_computation.8 | async-start | bytes 270336 | tf_op jit(solution)/shard_map/reduce_scatter | solution.py:343
  1082.9 5.9 copy-start.25
  1090.9 3.2 copy-start.22
  1095.5 2.0 copy-start.7
  1095.5 2.0 copy-start.18
  1095.5 2.1 copy-start.20
  1097.6 3.4 copy-start.9
  1106.5 2.0 copy-start.7
  1112.3 181.8 %copy-start.2 = (bf16[5,256,256]{1,2,0:T(8,128)(2,1)S(1)}, bf16[5,256,256]{1,2,0:T(8,128)(2,1)}, u32[]{:S(2)}) copy-start(bf16[5,256,256]{1,2,0:T(8,128)(2,1)} %copy-done.1) | copy-start | bytes 1966084
  1112.3 181.8 %copy-start.4 = (bf16[1,256,640]{1,2,0:T(8,128)(2,1)S(1)}, bf16[1,256,640]{1,2,0:T(8,128)(2,1)}, u32[]{:S(2)}) copy-start(bf16[1,256,640]{1,2,0:T(8,128)(2,1)} %copy-done.3) | copy-start | bytes 983044
  1112.4 176.4 %reduce-scatter.5.cloned.1.call-start = ((), (), s32[]{:S(2)}) async-start(), calls=%async_computation.9 | async-start | bytes 270336 | tf_op jit(solution)/shard_map/reduce_scatter | solution.py:346
  1114.4 8.3 all-to-all-start.3
  1122.7 78.1 %all-to-all-start.1 = ((bf16[8,2,640]{2,1,0:T(2,128)(2,1)}), bf16[8,2,640]{2,1,0:T(2,128)(2,1)S(1)}, u32[]{:S(2)}, u32[]{:S(2)}) async-start(bf16[8,2,640]{2,1,0:T(2,128)(2,1)} %all_to_all.83), calls=%async_computation.1 | async-start | bytes 40960 | tf_op jit(solution)/shard_map/all_to_all | solution.py:351
  1200.8 89.3 %all-to-all-start.4 = ((bf16[8,2,128]{2,1,0:T(2,128)(2,1)}), bf16[8,2,128]{2,1,0:T(2,128)(2,1)S(1)}, u32[]{:S(2)}, u32[]{:S(2)}) async-start(bf16[8,2,128]{2,1,0:T(2,128)(2,1)} %bitcast.140), calls=%async_computation.5 | async-start | bytes 8192 | tf_op jit(solution)/shard_map/all_to_all | solution.py:361
  1205.9 90.0 %copy-start.11 = (bf16[256,1,5,128]{0,3,2,1:T(8,128)(2,1)S(1)}, bf16[256,1,5,128]{0,3,2,1:T(8,128)(2,1)}, u32[]{:S(2)}) copy-start(bf16[256,1,5,128]{0,3,2,1:T(8,128)(2,1)} %get-tuple-element.859) | copy-start | bytes 983044
  1290.1 9.0 all-to-all-start.5
  (25 other events, 29.3 us)
Sparse Core Ops, SparseCore 0:
  9.8 533.6 all-gather.4
  545.3 525.5 all-gather.6
  1112.5 86.9 reduce-scatter.2
  1203.1 85.6 reduce-scatter.4
where the time goes:
time: 1310 us
  waiting for transfers between devices  1200 us (92%)
  local copies, waits for them, and re-layouts  31.5 us (2%)
  starting transfers between devices  25.4 us (2%)
  matrix products  15.2 us (1%)
  between operations  14.8 us (1%)
    all_gather x1, waiting for transfers between devices, body(): lax.all_gather(prompt_v, ('seq', 'head'), axis=0, tiled=True)  524 us
    all_gather x1, waiting for transfers between devices, body(): lax.all_gather(prompt_k, ('seq', 'head'), axis=0, tiled=True)  514 us
    reduce_scatter x1, waiting for transfers between devices, body(): lax.psum_scatter(value_terms.reshape(prompt_total, group_width), 'seq', s...  82.9 us
    reduce_scatter x1, waiting for transfers between devices, body(): lax.psum_scatter(key_terms.reshape(prompt_total, group_width), 'seq', sca...  73.4 us
  transfers between devices with their start and end apart: 10, of which 8 were waited for; matrix products, arithmetic and copies ran while one was open for 1% of the time, Pallas kernels for 0%

commit v1 on v0

v1 whole, which is shorter than its diff:
```python
import math

import jax
import jax.numpy as jnp
from jax import lax
from jax.experimental import pallas as pl
from jax.experimental.pallas import tpu as pltpu
from jax.sharding import Mesh, PartitionSpec as P

HEADS = 40
KV_HEADS = 8
HEAD_DIM = 128
GROUP = HEADS // KV_HEADS
PROMPT = 512
ANS_LEN = 256
HALF = PROMPT // 2
PAIRS = 2 * GROUP
PEERS = 16
NEG = -1e30
SCALING = 1.0 / math.sqrt(HEAD_DIM)
SCALE2 = SCALING / math.log(2.0)
SEQ_AXES = ("y", "zh", "c")
HEAD_AXES = ("x", "zl")
SAME_CORE = ("y", "zh", "x", "zl")
VMEM = pl.BlockSpec(memory_space=pltpu.VMEM)
SMEM = pl.BlockSpec(memory_space=pltpu.SMEM)


def dot(a, b, dims):
    return lax.dot_general(a, b, (dims, ((), ())), preferred_element_type=jnp.float32)


NT = ((1,), (1,))
NN = ((1,), (0,))


def cols(i):
    return slice(i * HEAD_DIM, (i + 1) * HEAD_DIM)


def pack_kernel(q_ref, g_ref, k_ref, v_ref, o_ref):
    q = q_ref[...].astype(jnp.float32)
    g = g_ref[...].astype(jnp.float32)
    zero = jnp.zeros((2, HEAD_DIM), jnp.bfloat16)
    rows = [
        jnp.concatenate([q[r : r + 1], g[r : r + 1]], axis=0).astype(jnp.bfloat16)
        for r in range(2)
    ]
    for h in range(KV_HEADS):
        k = k_ref[:, cols(h)]
        v = v_ref[:, cols(h)]
        for yz in range(PEERS):
            o_ref[yz * KV_HEADS + h, :, cols(0)] = k
            o_ref[yz * KV_HEADS + h, :, cols(1)] = v
            if yz < PAIRS:
                pair = rows[yz // GROUP][:, cols(h * GROUP + yz % GROUP)]
            else:
                pair = zero
            o_ref[yz * KV_HEADS + h, :, cols(2)] = pair


def unpack_kernel(x_ref, out_ref, dq_ref, dk_ref, dv_ref):
    for h in range(KV_HEADS):
        total = jnp.zeros((2, 2 * HEAD_DIM), jnp.float32)
        for yz in range(PEERS):
            total += x_ref[yz * KV_HEADS + h, :, : 2 * HEAD_DIM].astype(jnp.float32)
        dk_ref[:, cols(h)] = total[:, :HEAD_DIM].astype(jnp.bfloat16)
        dv_ref[:, cols(h)] = total[:, HEAD_DIM:].astype(jnp.bfloat16)
        for n in range(GROUP):
            first = x_ref[n * KV_HEADS + h, :, cols(2)].astype(jnp.float32)
            second = x_ref[(GROUP + n) * KV_HEADS + h, :, cols(2)].astype(jnp.float32)
            at = cols(h * GROUP + n)
            out_ref[:, at] = jnp.concatenate([first[:1], second[:1]], axis=0).astype(jnp.bfloat16)
            dq_ref[:, at] = jnp.concatenate([first[1:], second[1:]], axis=0).astype(jnp.bfloat16)


def deinterleave(shape, row_axis):
    i = lax.broadcasted_iota(jnp.int32, shape, row_axis)
    j = lax.broadcasted_iota(jnp.int32, shape, 1 - row_axis)
    source = jnp.where(i < HALF // 2, 2 * i, 2 * i - HALF + 1)
    return (source == j).astype(jnp.bfloat16)


def attend(keys, values, keys_t, values_t, queries, grads, mask):
    scores = mask(dot(keys, queries, NT))
    top = jnp.max(scores, axis=0, keepdims=True)
    weights = jnp.exp2(scores * SCALE2 - top * SCALE2)
    weights = weights * (1.0 / jnp.sum(weights, axis=0, keepdims=True))
    weights_low = weights.astype(jnp.bfloat16)
    out_t = dot(values_t, weights_low, NN)
    product = weights * dot(values, grads, NT)
    delta = jnp.sum(product, axis=0, keepdims=True)
    score_grad = (product - weights * delta).astype(jnp.bfloat16)
    query_grad_t = dot(keys_t, score_grad, NN) * SCALING
    key_grad = dot(score_grad, queries, NN)
    value_grad = dot(weights_low, grads, NN)
    return out_t, query_grad_t, key_grad, value_grad


def main_kernel(
    info_ref, last_ref, own_ref, sib_ref, aq_ref, ak_ref, av_ref, ag_ref,
    aout_ref, adq_ref, adk_ref, adv_ref, down_ref, dsib_ref, pair_ref,
    dk_ref, dv_ref,
):
    length = info_ref[0]
    core = info_ref[1]
    keys = jnp.concatenate([own_ref[:, cols(0)], sib_ref[:, cols(0)], ak_ref[...]], axis=0)
    values = jnp.concatenate([own_ref[:, cols(1)], sib_ref[:, cols(1)], av_ref[...]], axis=0)
    keys_t = keys.T
    values_t = values.T

    moved = dot(deinterleave((HALF, HALF), 0), own_ref[:, cols(2)], NN).astype(jnp.bfloat16)
    j = lax.broadcasted_iota(jnp.int32, (PROMPT, HALF // 2), 0)
    side = jnp.where(j < HALF, core, 1 - core)
    k_pos = ((j & (HALF - 1)) >> 4) * 32 + side * 16 + (j & 15)

    def prompt_mask(scores):
        return jnp.where(k_pos <= last_ref[...], scores, NEG)

    out_t, dq_t, dk, dv = attend(
        keys[:PROMPT], values[:PROMPT], keys_t[:, :PROMPT], values_t[:, :PROMPT],
        moved[: HALF // 2], moved[HALF // 2 :], prompt_mask,
    )
    both = jnp.concatenate([out_t.T, dq_t.T], axis=0).astype(jnp.bfloat16)
    pair_ref[...] = dot(deinterleave((HALF, HALF), 1), both, NN).astype(jnp.bfloat16)
    dk_ref[:PROMPT] = dk
    dv_ref[:PROMPT] = dv
    dk_ref[PROMPT:] = jnp.zeros((ANS_LEN, HEAD_DIM), jnp.float32)
    dv_ref[PROMPT:] = jnp.zeros((ANS_LEN, HEAD_DIM), jnp.float32)

    u = lax.broadcasted_iota(jnp.int32, (ANS_LEN, ANS_LEN), 0)
    t = lax.broadcasted_iota(jnp.int32, (ANS_LEN, ANS_LEN), 1)
    seen = (u <= t) & (u < length)
    live_row = lax.broadcasted_iota(jnp.int32, (ANS_LEN, HEAD_DIM), 0) < length

    def answer_mask(scores):
        return jnp.concatenate(
            [scores[:PROMPT], jnp.where(seen, scores[PROMPT:], NEG)], axis=0
        )

    for n in range(GROUP):
        queries = aq_ref[:, cols(n)]
        grads = ag_ref[:, cols(n)]
        grads = jnp.where(live_row, grads, jnp.zeros_like(grads))
        out_t, dq_t, dk, dv = attend(
            keys, values, keys_t, values_t, queries, grads, answer_mask
        )
        aout_ref[:, cols(n)] = jnp.where(live_row, out_t.T, 0.0).astype(jnp.bfloat16)
        adq_ref[:, cols(n)] = dq_t.T.astype(jnp.bfloat16)
        dk_ref[...] += dk
        dv_ref[...] += dv
    adk_ref[...] = (dk_ref[PROMPT:] * SCALING).astype(jnp.bfloat16)
    adv_ref[...] = dv_ref[PROMPT:].astype(jnp.bfloat16)
    down_ref[:, cols(0)] = dk_ref[:HALF] * SCALING
    down_ref[:, cols(1)] = dv_ref[:HALF]
    dsib_ref[:, cols(0)] = (dk_ref[HALF:PROMPT] * SCALING).astype(jnp.bfloat16)
    dsib_ref[:, cols(1)] = dv_ref[HALF:PROMPT].astype(jnp.bfloat16)


def call(kernel, out_shape, specs, scratch=(), flops=0, moved=0):
    return pl.pallas_call(
        kernel,
        out_shape=out_shape,
        in_specs=specs,
        out_specs=jax.tree.map(lambda _: VMEM, out_shape),
        scratch_shapes=list(scratch),
        cost_estimate=pl.CostEstimate(flops=flops, bytes_accessed=moved, transcendentals=0),
        compiler_params=pltpu.CompilerParams(vmem_limit_bytes=48 * 1024 * 1024),
    )


def bf16(*shape):
    return jax.ShapeDtypeStruct(shape, jnp.bfloat16)


def body(
    prompt_q, prompt_k, prompt_v, prompt_grad, segment_ids,
    answer_q, answer_k, answer_v, answer_grad, answer_lengths,
):
    core = lax.axis_index("c").astype(jnp.int32)
    peer = lax.axis_index(("y", "zh")).astype(jnp.int32)
    wide = HEADS * HEAD_DIM
    narrow = KV_HEADS * HEAD_DIM
    packed = call(pack_kernel, bf16(128, 2, 3 * HEAD_DIM), [VMEM] * 4)(
        prompt_q, prompt_grad, prompt_k, prompt_v
    )
    own = lax.all_to_all(packed, SAME_CORE, split_axis=0, concat_axis=0, tiled=True)
    own = own.reshape(HALF, 3 * HEAD_DIM)
    sibling = lax.ppermute(own, "c", [(0, 1), (1, 0)])

    row = jnp.where(peer >= GROUP, 1, 0)
    segments = lax.dynamic_slice(
        segment_ids.reshape(PEERS, 2, KV_HEADS, 2), (0, core, 0, row), (PEERS, 1, KV_HEADS, 1)
    ).reshape(1, HALF // 2)
    last = jnp.sum(
        (segment_ids[:, None] <= segments).astype(jnp.int32), axis=0, keepdims=True
    ) - 1
    info = jnp.stack([answer_lengths[0], core])

    a_out, a_dq, a_dk, a_dv, d_own, d_sib, pair = call(
        main_kernel,
        (
            bf16(ANS_LEN, GROUP * HEAD_DIM), bf16(ANS_LEN, GROUP * HEAD_DIM),
            bf16(ANS_LEN, HEAD_DIM), bf16(ANS_LEN, HEAD_DIM),
            jax.ShapeDtypeStruct((HALF, 2 * HEAD_DIM), jnp.float32),
            bf16(HALF, 2 * HEAD_DIM), bf16(HALF, HEAD_DIM),
        ),
        [SMEM] + [VMEM] * 7,
        scratch=[
            pltpu.VMEM((PROMPT + ANS_LEN, HEAD_DIM), jnp.float32),
            pltpu.VMEM((PROMPT + ANS_LEN, HEAD_DIM), jnp.float32),
        ],
        flops=1_600_000_000, moved=2_000_000,
    )(info, last, own, sibling, answer_q[0], answer_k[0], answer_v[0], answer_grad[0])

    d_mine = lax.ppermute(d_sib, "c", [(0, 1), (1, 0)])
    terms = (d_own + d_mine.astype(jnp.float32)).astype(jnp.bfloat16)
    back = jnp.concatenate([terms, pair], axis=1).reshape(128, 2, 3 * HEAD_DIM)
    back = lax.all_to_all(back, SAME_CORE, split_axis=0, concat_axis=0, tiled=True)
    p_out, p_dq, p_dk, p_dv = call(
        unpack_kernel, (bf16(2, wide), bf16(2, wide), bf16(2, narrow), bf16(2, narrow)), [VMEM]
    )(back)
    return (p_out, p_dq, p_dk, p_dv, a_out[None], a_dq[None], a_dk[None], a_dv[None])


def solution(mesh):
    grid = Mesh(mesh.devices.reshape(4, 4, 2, 4, 2), SEQ_AXES + HEAD_AXES)
    rows = P(SEQ_AXES + HEAD_AXES, None)
    answers = P(SEQ_AXES, None, HEAD_AXES)
    return jax.shard_map(
        body,
        mesh=grid,
        in_specs=(rows, rows, rows, rows, P(), answers, answers, answers, answers, P(SEQ_AXES)),
        out_specs=(rows, rows, rows, rows, answers, answers, answers, answers),
        check_vma=False,
    )
```

time: 1310 us -> 66.5 us (0.05)
  waiting for transfers between devices: 1200 us -> 12.6 us
  local copies, waits for them, and re-layouts: 31.5 us -> 3.65 us
  blocking collectives: 0 us -> 18.2 us
  matrix products: 15.2 us -> 0 us
  between operations: 14.8 us -> 1.46 us
    all_gather x2 -> x0, waiting for transfers between devices: 1040 us -> none  [the longest x1 524 us: body(): lax.all_gather(prompt_v, ('seq', 'head'), axis=0, tiled=True)]
    reduce_scatter x2 -> x0, waiting for transfers between devices: 156 us -> none  [the longest x1 82.9 us: body(): lax.psum_scatter(value_terms.reshape(prompt_total, group_width), 'seq', s...]
    all_to_all x0 -> x1, blocking collectives: none -> 18.2 us  [body(): lax.all_to_all(back, SAME_CORE, split_axis=0, concat_axis=0, tiled=True)]
    dot_general x27 -> x0, matrix products: 15.2 us -> none  [the longest x4 3.35 us: block_grads(): jnp.einsum('gnrc,cgd->rgnd', score_grad, keys_block, preferred_element_ty...]
  transfers between devices with their start and end apart: 10 -> 3, of which waited for: 8 -> 3; matrix products, arithmetic and copies ran while one was open for 1% -> 1% of each run, Pallas kernels for 0% -> 0%
where the time goes in v1:
time: 66.5 us; the launch traced here: 66.1 us
  starting transfers between devices  19.3 us (29%)
  blocking collectives  18.2 us (27%)
  waiting for transfers between devices  12.6 us (19%)
  Pallas kernels  10.6 us (16%)
  local copies, waits for them, and re-layouts  3.65 us (5%)
  between operations  1.46 us (2%)
    all_to_all x1, blocking collectives, body(): lax.all_to_all(back, SAME_CORE, split_axis=0, concat_axis=0, tiled=True)  18.2 us
    all_to_all x1, starting transfers between devices, body(): lax.all_to_all(packed, SAME_CORE, split_axis=0, concat_axis=0, tiled=True)  16.5 us
    all_to_all x1, waiting for transfers between devices, body(): lax.all_to_all(packed, SAME_CORE, split_axis=0, concat_axis=0, tiled=True)  10.6 us
    pallas_call x1, Pallas kernels, body(): call(main_kernel, (bf16(ANS_LEN, GROUP * HEAD_DIM), bf16(ANS_LEN, GROUP *...  9.08 us
    unnamed x18, local copies, waits for them, and re-layouts  2.85 us
    ppermute x1, starting transfers between devices, body(): sibling = lax.ppermute(own, 'c', [(0, 1), (1, 0)])  2.43 us
  transfers between devices with their start and end apart: 3, of which 3 were waited for; matrix products, arithmetic and copies ran while one was open for 1% of the time, Pallas kernels for 0%

profile of v1, /device:TPU:1, one launch (start us, length us, event | category | flops | bytes accessed | tf_op | source)
XLA Modules:
  0.0 66.1 jit_solution(8667006016542580)
XLA Ops:
  0.6 0.7 %copy-done = bf16[2,5120]{1,0:T(2,128)(2,1)S(1)} copy-done((bf16[2,5120]{1,0:T(2,128)(2,1)S(1)}, bf16[2,5120]{1,0:T(2,128)(2,1)}, u32[]{:S(2)}) %copy-start) | copy-done | bytes 20504
  1.4 0.7 %copy-done.1 = bf16[2,5120]{1,0:T(2,128)(2,1)S(1)} copy-done((bf16[2,5120]{1,0:T(2,128)(2,1)S(1)}, bf16[2,5120]{1,0:T(2,128)(2,1)}, u32[]{:S(2)}) %copy-start.1) | copy-done | bytes 20504
  2.1 0.7 %copy-done.2 = bf16[2,1024]{1,0:T(2,128)(2,1)S(1)} copy-done((bf16[2,1024]{1,0:T(2,128)(2,1)S(1)}, bf16[2,1024]{1,0:T(2,128)(2,1)}, u32[]{:S(2)}) %copy-start.2) | copy-done | bytes 4120
  2.8 0.7 %copy-done.3 = bf16[2,1024]{1,0:T(2,128)(2,1)S(1)} copy-done((bf16[2,1024]{1,0:T(2,128)(2,1)S(1)}, bf16[2,1024]{1,0:T(2,128)(2,1)}, u32[]{:S(2)}) %copy-start.3) | copy-done | bytes 4120
  3.5 0.8 %shard_map.161 = bf16[128,2,384]{2,1,0:T(2,128)(2,1)} custom-call(bf16[2,5120]{1,0:T(2,128)(2,1)S(1)} %copy-done, bf16[2,5120]{1,0:T(2,128)(2,1)S(1)} %copy-done.1, bf16[2,1024]{1,0:T(2,128)(2,1)S(1)} %copy-done.2, bf16[2,1024]{1,0:T(2,128)(2,1)S(1)} %copy-done.3), custom_call_target="tpu_custom_call" | custom-call | tf_op jit(solution)/shard_map/pallas_call | solution.py:184
  4.3 16.5 %all-to-all-start = ((bf16[128,2,384]{2,1,0:T(2,128)(2,1)}), bf16[128,2,384]{2,1,0:T(2,128)(2,1)S(1)}, u32[]{:S(2)}, u32[]{:S(2)}) async-start(bf16[128,2,384]{2,1,0:T(2,128)(2,1)} %shard_map.161), calls=%async_computation | async-start | bytes 393216 | tf_op jit(solution)/shard_map/all_to_all | solution.py:187
  20.7 0.0 copy-start.8
  20.8 0.0 copy-start.4
  20.8 0.0 copy-start.5
  21.5 0.1 reshape.38
  21.7 0.4 dynamic-slice_reduce_fusion
  22.1 0.1 le.16
  22.2 0.1 pad_add_fusion.info_ref
  22.3 0.1 convert_reduce_fusion
  22.4 10.6 %all-to-all-done = bf16[128,2,384]{2,1,0:T(2,128)(2,1)S(1)} async-done(((bf16[128,2,384]{2,1,0:T(2,128)(2,1)}), bf16[128,2,384]{2,1,0:T(2,128)(2,1)S(1)}, u32[]{:S(2)}, u32[]{:S(2)}) %all-to-all-start) | async-done | bytes 196640 | tf_op jit(solution)/shard_map/all_to_all | solution.py:187
  33.0 0.1 reshape.39.own_ref
  33.1 2.4 %collective-permute-start = (bf16[256,384]{1,0:T(8,128)(2,1)S(1)}, bf16[256,384]{1,0:T(8,128)(2,1)S(1)}, u32[]{:S(2)}, u32[]{:S(2)}) collective-permute-start(bf16[256,384]{1,0:T(8,128)(2,1)S(1)} %reshape.39.own_ref), channel_id=1, source_target_pairs={{0,8},{8,0},{1,9},{9,1},{2,10},{10,2},{3,11},{11,3},{4,12},{12,4},... | collective-permute-start | bytes 589832 | tf_op jit(solution)/shard_map/ppermute | solution.py:189
  35.5 1.1 %collective-permute-done.sib_ref = bf16[256,384]{1,0:T(8,128)(2,1)S(1)} collective-permute-done((bf16[256,384]{1,0:T(8,128)(2,1)S(1)}, bf16[256,384]{1,0:T(8,128)(2,1)S(1)}, u32[]{:S(2)}, u32[]{:S(2)}) %collective-permute-start) | collective-permute-done | bytes 196640 | tf_op jit(solution)/shard_map/ppermute | solution.py:189
  36.6 9.1 %shard_map.162 = (bf16[256,640]{1,0:T(8,128)(2,1)}, bf16[256,640]{1,0:T(8,128)(2,1)}, bf16[256,128]{1,0:T(8,128)(2,1)}, bf16[256,128]{1,0:T(8,128)(2,1)}, f32[25...) custom-call(s32[2]{0:T(128)S(1)} %pad_add_fusion.info_ref, ...), custom_call_target="tpu_custom_call" | custom-call | flops 1600000000 | bytes 2000000 | tf_op jit(solution)/shard_map/pallas_call | solution.py:200
  45.7 0.4 collective-permute-start.1
  46.1 1.0 %collective-permute-done.1 = bf16[256,256]{1,0:T(8,128)(2,1)S(1)} collective-permute-done((bf16[256,256]{1,0:T(8,128)(2,1)S(1)}, bf16[256,256]{1,0:T(8,128)(2,1)S(1)}, u32[]{:S(2)}, u32[]{:S(2)}) %collective-permute-start.1) | collective-permute-done | bytes 131104 | tf_op jit(solution)/shard_map/ppermute | solution.py:216
  47.1 0.1 reshape.40
  47.2 18.2 %all_to_all.10.x_ref = bf16[128,2,384]{2,1,0:T(2,128)(2,1)S(1)} all-to-all(bf16[128,2,384]{2,1,0:T(2,128)(2,1)S(1)} %reshape.40), channel_id=1, replica_groups=mesh['y'=4,'zh'=4,'c'=2,'x'=4,'zl'=2] {'y','zh','x','zl'}, dimensions={0} | all-to-all | bytes 393216 | tf_op jit(solution)/shard_map/all_to_all | solution.py:219
  65.4 0.7 %shard_map.163 = (bf16[2,5120]{1,0:T(2,128)(2,1)}, bf16[2,5120]{1,0:T(2,128)(2,1)}, bf16[2,1024]{1,0:T(2,128)(2,1)}, bf16[2,1024]{1,0:T(2,128)(2,1)}) custom-call(bf16[128,2,384]{2,1,0:T(2,128)(2,1)S(1)} %all_to_all.10.x_ref), custom_call_target="tpu_custom_call" | custom-call | tf_op jit(solution)/shard_map/pallas_call | solution.py:220
  (14 shorter events, 0.1 us)
Async XLA Ops:
  0.6 0.7 %copy-start = (bf16[2,5120]{1,0:T(2,128)(2,1)S(1)}, bf16[2,5120]{1,0:T(2,128)(2,1)}, u32[]{:S(2)}) copy-start(bf16[2,5120]{1,0:T(2,128)(2,1)} %q_ref.1) | copy-start | bytes 61444
  1.4 0.7 %copy-start.1 = (bf16[2,5120]{1,0:T(2,128)(2,1)S(1)}, bf16[2,5120]{1,0:T(2,128)(2,1)}, u32[]{:S(2)}) copy-start(bf16[2,5120]{1,0:T(2,128)(2,1)} %g_ref.1) | copy-start | bytes 61444
  2.1 0.7 %copy-start.2 = (bf16[2,1024]{1,0:T(2,128)(2,1)S(1)}, bf16[2,1024]{1,0:T(2,128)(2,1)}, u32[]{:S(2)}) copy-start(bf16[2,1024]{1,0:T(2,128)(2,1)} %k_ref.1) | copy-start | bytes 12292
  2.8 0.7 %copy-start.3 = (bf16[2,1024]{1,0:T(2,128)(2,1)S(1)}, bf16[2,1024]{1,0:T(2,128)(2,1)}, u32[]{:S(2)}) copy-start(bf16[2,1024]{1,0:T(2,128)(2,1)} %v_ref.1) | copy-start | bytes 12292
  4.3 32.3 %copy-start.6 = (bf16[1,256,128]{2,1,0:T(8,128)(2,1)S(1)}, bf16[1,256,128]{2,1,0:T(8,128)(2,1)}, u32[]{:S(2)}) copy-start(bf16[1,256,128]{2,1,0:T(8,128)(2,1)} %param.16) | copy-start | bytes 196612
  4.3 32.3 %copy-start.7 = (bf16[1,256,128]{2,1,0:T(8,128)(2,1)S(1)}, bf16[1,256,128]{2,1,0:T(8,128)(2,1)}, u32[]{:S(2)}) copy-start(bf16[1,256,128]{2,1,0:T(8,128)(2,1)} %param.17) | copy-start | bytes 196612
  4.3 28.7 %all-to-all-start = ((bf16[128,2,384]{2,1,0:T(2,128)(2,1)}), bf16[128,2,384]{2,1,0:T(2,128)(2,1)S(1)}, u32[]{:S(2)}, u32[]{:S(2)}) async-start(bf16[128,2,384]{2,1,0:T(2,128)(2,1)} %shard_map.161), calls=%async_computation | async-start | bytes 393216 | tf_op jit(solution)/shard_map/all_to_all | solution.py:187
  20.7 0.8 %copy-start.8 = (s32[512]{0:T(512)S(1)}, s32[512]{0:T(512)}, u32[]{:S(2)}) copy-start(s32[512]{0:T(512)} %param.14) | copy-start | bytes 6148
  20.8 15.8 %copy-start.4 = (bf16[1,256,640]{2,1,0:T(8,128)(2,1)S(1)}, bf16[1,256,640]{2,1,0:T(8,128)(2,1)}, u32[]{:S(2)}) copy-start(bf16[1,256,640]{2,1,0:T(8,128)(2,1)} %param.15) | copy-start | bytes 983044
  20.8 15.8 %copy-start.5 = (bf16[1,256,640]{2,1,0:T(8,128)(2,1)S(1)}, bf16[1,256,640]{2,1,0:T(8,128)(2,1)}, u32[]{:S(2)}) copy-start(bf16[1,256,640]{2,1,0:T(8,128)(2,1)} %param.18) | copy-start | bytes 983044
  33.1 3.5 %collective-permute-start = (bf16[256,384]{1,0:T(8,128)(2,1)S(1)}, bf16[256,384]{1,0:T(8,128)(2,1)S(1)}, u32[]{:S(2)}, u32[]{:S(2)}) collective-permute-start(bf16[256,384]{1,0:T(8,128)(2,1)S(1)} %reshape.39.own_ref), channel_id=1, source_target_pairs={{0,8},{8,0},{1,9},{9,1},{2,10},{10,2},{3,11},{11,3},{4,12},{12,4},... | collective-permute-start | bytes 589832 | tf_op jit(solution)/shard_map/ppermute | solution.py:189
  45.7 1.4 %collective-permute-start.1 = (bf16[256,256]{1,0:T(8,128)(2,1)S(1)}, bf16[256,256]{1,0:T(8,128)(2,1)S(1)}, u32[]{:S(2)}, u32[]{:S(2)}) collective-permute-start(bf16[256,256]{1,0:T(8,128)(2,1)S(1)} %get-tuple-element.20), channel_id=1, source_target_pairs={{0,8},{8,0},{1,9},{9,1},{2,10},{10,2},{3,11},{11,3},{4,12},{12,4},... | collective-permute-start | bytes 393224 | tf_op jit(solution)/shard_map/ppermute | solution.py:216

commit v2 on v1

v2 whole, which is shorter than its diff:
```python
import math

import jax
import jax.numpy as jnp
from jax import lax
from jax.experimental import pallas as pl
from jax.experimental.pallas import tpu as pltpu
from jax.sharding import Mesh, PartitionSpec as P

HEADS = 40
KV_HEADS = 8
HEAD_DIM = 128
GROUP = HEADS // KV_HEADS
PROMPT = 512
ANS_LEN = 256
HALF = PROMPT // 2
PAIRS = 2 * GROUP
PEERS = 16
SENDERS = 128
ROWS = GROUP * ANS_LEN
ALL = ROWS + SENDERS
NEG = -1e30
SCALING = 1.0 / math.sqrt(HEAD_DIM)
SCALE2 = SCALING / math.log(2.0)
SEQ_AXES = ("y", "zh", "c")
HEAD_AXES = ("x", "zl")
SAME_CORE = ("y", "zh", "x", "zl")
OTHER_CORE = [(0, 1), (1, 0)]
VMEM = pl.BlockSpec(memory_space=pltpu.VMEM)
SMEM = pl.BlockSpec(memory_space=pltpu.SMEM)
HBM = pl.BlockSpec(memory_space=pltpu.HBM)
NT = ((1,), (1,))
NN = ((1,), (0,))
BF16 = jnp.bfloat16
F32 = jnp.float32


def dot(a, b, dims):
    return lax.dot_general(a, b, (dims, ((), ())), preferred_element_type=F32)


def cols(i):
    return slice(i * HEAD_DIM, (i + 1) * HEAD_DIM)


def head(n):
    return slice(n * ANS_LEN, min((n + 1) * ANS_LEN, ALL))


def pack_kernel(q_hbm, g_hbm, k_hbm, v_hbm, o_ref, q_ref, g_ref, k_ref, v_ref, sems):
    pairs = ((k_hbm, k_ref), (v_hbm, v_ref), (q_hbm, q_ref), (g_hbm, g_ref))
    copies = [pltpu.make_async_copy(a, b, sems.at[i]) for i, (a, b) in enumerate(pairs)]
    for copy in copies:
        copy.start()
    for copy in copies:
        copy.wait()
    q = q_ref[...].astype(F32)
    g = g_ref[...].astype(F32)
    zero = jnp.zeros((2, HEAD_DIM), BF16)
    rows = [jnp.concatenate([q[r : r + 1], g[r : r + 1]], axis=0).astype(BF16) for r in range(2)]
    for h in range(KV_HEADS):
        k = k_ref[:, cols(h)]
        v = v_ref[:, cols(h)]
        for yz in range(PEERS):
            o_ref[yz * KV_HEADS + h, :, cols(0)] = k
            o_ref[yz * KV_HEADS + h, :, cols(1)] = v
            if yz < PAIRS:
                pair = rows[yz // GROUP][:, cols(h * GROUP + yz % GROUP)]
            else:
                pair = zero
            o_ref[yz * KV_HEADS + h, :, cols(2)] = pair


def unpack_kernel(x_ref, out_ref, dq_ref, dk_ref, dv_ref):
    for h in range(KV_HEADS):
        total = jnp.zeros((2, 2 * HEAD_DIM), F32)
        for yz in range(PEERS):
            total += x_ref[yz * KV_HEADS + h, :, : 2 * HEAD_DIM].astype(F32)
        dk_ref[:, cols(h)] = total[:, :HEAD_DIM].astype(BF16)
        dv_ref[:, cols(h)] = total[:, HEAD_DIM:].astype(BF16)
        for n in range(GROUP):
            first = x_ref[n * KV_HEADS + h, :, cols(2)].astype(F32)
            second = x_ref[(GROUP + n) * KV_HEADS + h, :, cols(2)].astype(F32)
            at = cols(h * GROUP + n)
            out_ref[:, at] = jnp.concatenate([first[:1], second[:1]], axis=0).astype(BF16)
            dq_ref[:, at] = jnp.concatenate([first[1:], second[1:]], axis=0).astype(BF16)


def post_kernel(own_ref, other_ref, pair_ref, o_ref):
    total = (own_ref[...] + other_ref[...].astype(F32)).astype(BF16)
    o_ref[:, :, : 2 * HEAD_DIM] = total.reshape(SENDERS, 2, 2 * HEAD_DIM)
    o_ref[:, :, 2 * HEAD_DIM :] = pair_ref[...].reshape(SENDERS, 2, HEAD_DIM)


def deinterleave(row_axis):
    i = lax.broadcasted_iota(jnp.int32, (HALF, HALF), row_axis)
    j = lax.broadcasted_iota(jnp.int32, (HALF, HALF), 1 - row_axis)
    source = jnp.where(i < SENDERS, 2 * i, 2 * i - HALF + 1)
    return (source == j).astype(BF16)


def seen_by(length):
    u = lax.broadcasted_iota(jnp.int32, (ANS_LEN, ANS_LEN), 0)
    t = lax.broadcasted_iota(jnp.int32, (ANS_LEN, ANS_LEN), 1)
    return (u <= t) & (u < length)


def live_rows(length):
    return lax.broadcasted_iota(jnp.int32, (ANS_LEN, HEAD_DIM), 0) < length


def column_sum(x):
    return jnp.sum(x, axis=0, keepdims=True)


def column_max(x):
    return jnp.max(x, axis=0, keepdims=True)


def own_kernel(
    len_ref, seg_hbm, aq_hbm, ak_hbm, av_hbm, ag_hbm,
    q_ref, g_ref, stat_ref, bias_ref,
    seg_ref, raw_ref, k_ref, v_ref, sems,
):
    pairs = [(seg_hbm, seg_ref), (ak_hbm, k_ref), (av_hbm, v_ref)]
    for n in range(GROUP):
        rows = pl.ds(n * ANS_LEN, ANS_LEN)
        at = pl.ds(n * HEAD_DIM, HEAD_DIM)
        pairs.append((aq_hbm.at[:, at], q_ref.at[rows, :]))
        pairs.append((ag_hbm.at[:, at], raw_ref.at[rows, :]))
    copies = [pltpu.make_async_copy(a, b, sems.at[i]) for i, (a, b) in enumerate(pairs)]
    for copy in copies:
        copy.start()
    length = len_ref[0]
    core = lax.axis_index("c")
    row = jnp.where(lax.axis_index("y") * 4 + lax.axis_index("zh") >= GROUP, 1, 0)

    shape = (PROMPT, PROMPT)
    j = lax.broadcasted_iota(jnp.int32, shape, 0)
    side = jnp.where(j < HALF, core, 1 - core)
    at = ((j & (HALF - 1)) >> 4) * 32 + side * 16 + (j & 15)
    key_pick = (at == lax.broadcasted_iota(jnp.int32, shape, 1)).astype(BF16)
    shape = (SENDERS, PROMPT)
    i = lax.broadcasted_iota(jnp.int32, shape, 0)
    at = (i >> 3) * 32 + core * 16 + (i & 7) * 2 + row
    row_pick = (at == lax.broadcasted_iota(jnp.int32, shape, 1)).astype(BF16)
    copies[0].wait()
    segments = jnp.broadcast_to(seg_ref[...].astype(F32), (SENDERS, PROMPT)).astype(BF16)
    key_segments = dot(key_pick, segments, NT)
    row_segments = dot(segments, row_pick, NT)[:1]
    bias_ref[...] = jnp.where(key_segments <= row_segments, 0.0, NEG)

    seen = seen_by(length)
    live_row = live_rows(length)
    for copy in copies[1:]:
        copy.wait()
    keys = k_ref[...]
    values = v_ref[...]
    for n in range(GROUP):
        grads = raw_ref[head(n)]
        grads = jnp.where(live_row, grads, jnp.zeros_like(grads))
        g_ref[head(n)] = grads
        scores = jnp.where(seen, dot(keys, q_ref[head(n)], NT), NEG)
        top = column_max(scores)
        weights = jnp.exp2(scores * SCALE2 - top * SCALE2)
        stat_ref[n : n + 1] = top
        stat_ref[8 + n : 9 + n] = column_sum(weights)
        stat_ref[16 + n : 17 + n] = column_sum(weights * dot(values, grads, NT))


def near_kernel(
    bias_ref, own_ref, q_ref, g_ref, stat_ref,
    e_ref, far_bias_ref, moved_ref, stat2_ref, q2_ref, g2_ref,
):
    keys = own_ref[:, cols(0)]
    values = own_ref[:, cols(1)]
    moved_ref[...] = dot(deinterleave(0), own_ref[:, cols(2)], NN).astype(BF16)
    far_bias_ref[...] = bias_ref[HALF:]
    q2_ref[...] = q_ref[...]
    g2_ref[...] = g_ref[...]
    for n in range(GROUP + 1):
        if n < GROUP:
            scores = dot(keys, q_ref[head(n)], NT)
            prob_grad = dot(values, g_ref[head(n)], NT)
            old_top = stat_ref[n : n + 1]
            top = jnp.maximum(column_max(scores), old_top)
        else:
            scores = dot(keys, moved_ref[:SENDERS], NT) + bias_ref[:HALF]
            prob_grad = dot(values, moved_ref[SENDERS:], NT)
            top = column_max(scores)
        weights = jnp.exp2(scores * SCALE2 - top * SCALE2)
        total = column_sum(weights)
        moment = column_sum(weights * prob_grad)
        if n < GROUP:
            shift = jnp.exp2((old_top - top) * SCALE2)
            total += stat_ref[8 + n : 9 + n] * shift
            moment += stat_ref[16 + n : 17 + n] * shift
        e_ref[:, head(n)] = weights
        wide = slice(0, weights.shape[1])
        stat2_ref[n : n + 1, wide] = top
        stat2_ref[8 + n : 9 + n, wide] = total
        stat2_ref[16 + n : 17 + n, wide] = moment


def far_kernel(
    bias_ref, own_ref, sib_ref, q_ref, g_ref, e_ref, moved_ref, stat_ref,
    dsib_ref, w_ref, ds_ref, stat2_ref,
):
    keys = sib_ref[:, cols(0)]
    values = sib_ref[:, cols(1)]
    near_values = own_ref[:, cols(1)]
    for n in range(GROUP + 1):
        if n < GROUP:
            scores = dot(keys, q_ref[head(n)], NT)
            grads = g_ref[head(n)]
        else:
            scores = dot(keys, moved_ref[:SENDERS], NT) + bias_ref[...]
            grads = moved_ref[SENDERS:]
        prob_grad = dot(values, grads, NT)
        wide = slice(0, scores.shape[1])
        old_top = stat_ref[n : n + 1, wide]
        top = jnp.maximum(column_max(scores), old_top)
        shift = jnp.exp2((old_top - top) * SCALE2)
        weights = jnp.exp2(scores * SCALE2 - top * SCALE2)
        total = column_sum(weights) + stat_ref[8 + n : 9 + n, wide] * shift
        moment = column_sum(weights * prob_grad) + stat_ref[16 + n : 17 + n, wide] * shift
        inverse = 1.0 / total
        delta = moment * inverse
        if n < GROUP:
            stat2_ref[n : n + 1] = top * SCALE2 + jnp.log2(total)
            stat2_ref[8 + n : 9 + n] = delta
        weights = weights * inverse
        w_ref[HALF:, head(n)] = weights.astype(BF16)
        ds_ref[HALF:, head(n)] = (weights * (prob_grad - delta)).astype(BF16)
        weights = e_ref[:, head(n)] * (shift * inverse)
        w_ref[:HALF, head(n)] = weights.astype(BF16)
        ds_ref[:HALF, head(n)] = (weights * (dot(near_values, grads, NT) - delta)).astype(BF16)
    dk, dv = key_terms(ds_ref[HALF:], w_ref[HALF:], q_ref, g_ref, moved_ref)
    dsib_ref[:, cols(0)] = dk.astype(BF16)
    dsib_ref[:, cols(1)] = dv.astype(BF16)


def key_terms(score_grad, weights, q_ref, g_ref, moved_ref):
    dk = dot(score_grad[:, :ROWS], q_ref[...], NN)
    dk += dot(score_grad[:, ROWS:], moved_ref[:SENDERS], NN)
    dv = dot(weights[:, :ROWS], g_ref[...], NN)
    dv += dot(weights[:, ROWS:], moved_ref[SENDERS:], NN)
    return dk * SCALING, dv


def mine_kernel(
    own_ref, sib_ref, q_ref, g_ref, moved_ref, w_ref, ds_ref, down_ref, pair_ref
):
    dk, dv = key_terms(ds_ref[:HALF], w_ref[:HALF], q_ref, g_ref, moved_ref)
    down_ref[:, cols(0)] = dk
    down_ref[:, cols(1)] = dv
    results = []
    for part, x_ref, factor in ((1, w_ref, 1.0), (0, ds_ref, SCALING)):
        turned = dot(own_ref[:, cols(part)].T, x_ref[:HALF, head(GROUP)], NN)
        turned += dot(sib_ref[:, cols(part)].T, x_ref[HALF:, head(GROUP)], NN)
        results.append((turned * factor).T)
    both = jnp.concatenate(results, axis=0).astype(BF16)
    pair_ref[...] = dot(deinterleave(1), both, NN).astype(BF16)


def rest_kernel(
    len_ref, aq_hbm, ak_hbm, av_hbm, ag_hbm, own_ref, sib_ref, w_ref, ds_ref, stat_ref,
    aout_ref, adq_ref, adk_ref, adv_ref, q_ref, k_ref, v_ref, g_ref, sems,
):
    pairs = ((aq_hbm, q_ref), (ak_hbm, k_ref), (av_hbm, v_ref), (ag_hbm, g_ref))
    copies = [pltpu.make_async_copy(a, b, sems.at[i]) for i, (a, b) in enumerate(pairs)]
    for copy in copies:
        copy.start()
    for copy in copies:
        copy.wait()
    length = len_ref[0]
    seen = seen_by(length)
    live_row = live_rows(length)
    keys = k_ref[...]
    values = v_ref[...]
    keys_t = keys.T
    values_t = values.T
    prompt_keys_t = jnp.concatenate([own_ref[:, cols(0)], sib_ref[:, cols(0)]], axis=0).T
    prompt_values_t = jnp.concatenate([own_ref[:, cols(1)], sib_ref[:, cols(1)]], axis=0).T
    dk = jnp.zeros((ANS_LEN, HEAD_DIM), F32)
    dv = jnp.zeros((ANS_LEN, HEAD_DIM), F32)
    for n in range(GROUP):
        queries = q_ref[:, cols(n)]
        grads = g_ref[:, cols(n)]
        grads = jnp.where(live_row, grads, jnp.zeros_like(grads))
        scores = jnp.where(seen, dot(keys, queries, NT), NEG)
        weights = jnp.exp2(scores * SCALE2 - stat_ref[n : n + 1])
        weights_low = weights.astype(BF16)
        product = dot(values, grads, NT) - stat_ref[8 + n : 9 + n]
        score_grad = (weights * product).astype(BF16)
        out_t = dot(prompt_values_t, w_ref[:, head(n)], NN) + dot(values_t, weights_low, NN)
        dq_t = dot(prompt_keys_t, ds_ref[:, head(n)], NN) + dot(keys_t, score_grad, NN)
        aout_ref[:, cols(n)] = jnp.where(live_row, out_t.T, 0.0).astype(BF16)
        adq_ref[:, cols(n)] = (dq_t * SCALING).T.astype(BF16)
        dk += dot(score_grad, queries, NN)
        dv += dot(weights_low, grads, NN)
    adk_ref[...] = (dk * SCALING).astype(BF16)
    adv_ref[...] = dv.astype(BF16)


def call(kernel, out_shape, specs, scratch=(), flops=0, moved=0, limit=16):
    return pl.pallas_call(
        kernel,
        out_shape=out_shape,
        in_specs=specs,
        out_specs=jax.tree.map(lambda _: VMEM, out_shape),
        scratch_shapes=list(scratch),
        cost_estimate=pl.CostEstimate(flops=flops, bytes_accessed=moved, transcendentals=0),
        compiler_params=pltpu.CompilerParams(vmem_limit_bytes=limit * 1024 * 1024),
    )


def bf16(*shape):
    return jax.ShapeDtypeStruct(shape, BF16)


def vmem(*shape, dtype=BF16):
    return pltpu.VMEM(shape, dtype)


def in_hbm(x):
    return pltpu.with_memory_space_constraint(x, pltpu.HBM)


def in_vmem(x):
    return pltpu.with_memory_space_constraint(x, pltpu.VMEM)


def body(
    prompt_q, prompt_k, prompt_v, prompt_grad, segment_ids,
    answer_q, answer_k, answer_v, answer_grad, answer_lengths,
):
    wide = HEADS * HEAD_DIM
    narrow = KV_HEADS * HEAD_DIM
    group = GROUP * HEAD_DIM
    packed = call(
        pack_kernel,
        bf16(SENDERS, 2, 3 * HEAD_DIM),
        [HBM] * 4,
        scratch=[
            pltpu.VMEM((2, wide), BF16), pltpu.VMEM((2, wide), BF16),
            pltpu.VMEM((2, narrow), BF16), pltpu.VMEM((2, narrow), BF16),
            pltpu.SemaphoreType.DMA((4,)),
        ],
        limit=4,
    )(in_hbm(prompt_q), in_hbm(prompt_grad), in_hbm(prompt_k), in_hbm(prompt_v))
    packed, answer_q = lax.optimization_barrier((packed, answer_q))
    own = lax.all_to_all(packed, SAME_CORE, split_axis=0, concat_axis=0, tiled=True)
    own = own.reshape(HALF, 3 * HEAD_DIM)

    queries, grads, stat, bias = call(
        own_kernel,
        (
            vmem(ROWS, HEAD_DIM), vmem(ROWS, HEAD_DIM), vmem(24, ANS_LEN, dtype=F32),
            vmem(PROMPT, SENDERS, dtype=F32),
        ),
        [SMEM] + [HBM] * 5,
        scratch=[
            pltpu.VMEM((1, PROMPT), jnp.int32), pltpu.VMEM((ROWS, HEAD_DIM), BF16),
            pltpu.VMEM((ANS_LEN, HEAD_DIM), BF16), pltpu.VMEM((ANS_LEN, HEAD_DIM), BF16),
            pltpu.SemaphoreType.DMA((3 + 2 * GROUP,)),
        ],
        flops=400_000_000, moved=2_000_000,
    )(
        answer_lengths, in_hbm(segment_ids.reshape(1, PROMPT)), in_hbm(answer_q[0]),
        in_hbm(answer_k[0]), in_hbm(answer_v[0]), in_hbm(answer_grad[0]),
    )
    own, stat = lax.optimization_barrier((own, stat))
    sibling = lax.ppermute(own, "c", OTHER_CORE)
    exps, bias, moved, stat, queries, grads = call(
        near_kernel,
        (
            vmem(HALF, ALL, dtype=F32), vmem(HALF, SENDERS, dtype=F32), vmem(HALF, HEAD_DIM),
            vmem(24, ANS_LEN, dtype=F32), vmem(ROWS, HEAD_DIM), vmem(ROWS, HEAD_DIM),
        ),
        [VMEM] * 5,
        flops=200_000_000, moved=2_000_000,
    )(bias, own, queries, grads, stat)
    d_sib, weights, score_grad, stat = call(
        far_kernel,
        (
            vmem(HALF, 2 * HEAD_DIM), vmem(PROMPT, ALL), vmem(PROMPT, ALL),
            vmem(16, ANS_LEN, dtype=F32),
        ),
        [VMEM] * 8,
        flops=400_000_000, moved=2_000_000,
    )(bias, own, sibling, queries, grads, exps, moved, stat)

    d_mine = lax.ppermute(d_sib, "c", OTHER_CORE)
    d_own, pair = call(
        mine_kernel,
        (vmem(HALF, 2 * HEAD_DIM, dtype=F32), vmem(HALF, HEAD_DIM)),
        [VMEM] * 7,
        flops=200_000_000, moved=2_000_000,
    )(own, sibling, queries, grads, moved, weights, score_grad)
    back = call(
        post_kernel, bf16(SENDERS, 2, 3 * HEAD_DIM), [VMEM] * 3, limit=4, moved=700_000
    )(d_own, d_mine, pair)
    back, stat = lax.optimization_barrier((back, stat))
    back = lax.all_to_all(back, SAME_CORE, split_axis=0, concat_axis=0, tiled=True)
    a_out, a_dq, a_dk, a_dv = call(
        rest_kernel,
        (
            bf16(ANS_LEN, group), bf16(ANS_LEN, group),
            bf16(ANS_LEN, HEAD_DIM), bf16(ANS_LEN, HEAD_DIM),
        ),
        [SMEM] + [HBM] * 4 + [VMEM] * 5,
        scratch=[
            pltpu.VMEM((ANS_LEN, group), BF16), pltpu.VMEM((ANS_LEN, HEAD_DIM), BF16),
            pltpu.VMEM((ANS_LEN, HEAD_DIM), BF16), pltpu.VMEM((ANS_LEN, group), BF16),
            pltpu.SemaphoreType.DMA((4,)),
        ],
        flops=700_000_000, moved=2_000_000,
    )(
        answer_lengths, in_hbm(answer_q[0]), in_hbm(answer_k[0]), in_hbm(answer_v[0]),
        in_hbm(answer_grad[0]), own, sibling, weights, score_grad, stat,
    )
    p_out, p_dq, p_dk, p_dv = call(
        unpack_kernel, (bf16(2, wide), bf16(2, wide), bf16(2, narrow), bf16(2, narrow)), [VMEM],
        limit=4,
    )(in_vmem(back))
    return (p_out, p_dq, p_dk, p_dv, a_out[None], a_dq[None], a_dk[None], a_dv[None])


def solution(mesh):
    grid = Mesh(mesh.devices.reshape(4, 4, 2, 4, 2), SEQ_AXES + HEAD_AXES)
    rows = P(SEQ_AXES + HEAD_AXES, None)
    answers = P(SEQ_AXES, None, HEAD_AXES)
    return jax.shard_map(
        body,
        mesh=grid,
        in_specs=(rows, rows, rows, rows, P(), answers, answers, answers, answers, P(SEQ_AXES)),
        out_specs=(rows, rows, rows, rows, answers, answers, answers, answers),
        check_vma=False,
    )
```

time: 66.5 us -> 58.6 us (0.88)
  blocking collectives: 18.2 us -> 0 us
  waiting for transfers between devices: 12.6 us -> 18.8 us
  starting transfers between devices: 19.3 us -> 25.4 us
  local copies, waits for them, and re-layouts: 3.65 us -> 0.75 us
  Pallas kernels: 10.6 us -> 12 us
    all_to_all x1 -> x0, blocking collectives: 18.2 us -> none  [body(): lax.all_to_all(back, SAME_CORE, split_axis=0, concat_axis=0, tiled=True)]
    all_to_all x0 -> x1, waiting for transfers between devices: none -> 8.69 us  [body(): lax.all_to_all(back, SAME_CORE, split_axis=0, concat_axis=0, tiled=True)]
    all_to_all x0 -> x1, starting transfers between devices: none -> 6.15 us  [body(): lax.all_to_all(back, SAME_CORE, split_axis=0, concat_axis=0, tiled=True)]
    unnamed x18 -> x2, local copies, waits for them, and re-layouts: 2.85 us -> 0.67 us
    ppermute x2, waiting for transfers between devices: 2.05 us -> 0.44 us  [the longest x1 0.35 us: body(): sibling = lax.ppermute(own, 'c', OTHER_CORE)]
    pallas_call x2 -> x7, Pallas kernels: 9.88 us -> 11.3 us  [the longest x1 4.16 us: body(): call(rest_kernel, (bf16(ANS_LEN, group), bf16(ANS_LEN, group), bf16(ANS_L...]
    all_to_all x1, waiting for transfers between devices: 10.6 us -> 9.63 us  [body(): lax.all_to_all(packed, SAME_CORE, split_axis=0, concat_axis=0, tiled=True)]
  transfers between devices with their start and end apart: 3 -> 4, of which waited for: 3 -> 4; matrix products, arithmetic and copies ran while one was open for 1% -> 0% of each run, Pallas kernels for 0% -> 13%
where the time goes in v2:
time: 58.6 us; the launch traced here: 58.3 us
  starting transfers between devices  25.4 us (43%)
  waiting for transfers between devices  18.8 us (32%)
  Pallas kernels  12 us (20%)
  between operations  1.35 us (2%)
  local copies, waits for them, and re-layouts  0.75 us (1%)
    all_to_all x1, starting transfers between devices, body(): lax.all_to_all(packed, SAME_CORE, split_axis=0, concat_axis=0, tiled=True)  16.3 us
    all_to_all x1, waiting for transfers between devices, body(): lax.all_to_all(packed, SAME_CORE, split_axis=0, concat_axis=0, tiled=True)  9.63 us
    all_to_all x1, waiting for transfers between devices, body(): lax.all_to_all(back, SAME_CORE, split_axis=0, concat_axis=0, tiled=True)  8.69 us
    all_to_all x1, starting transfers between devices, body(): lax.all_to_all(back, SAME_CORE, split_axis=0, concat_axis=0, tiled=True)  6.15 us
    pallas_call x1, Pallas kernels, body(): call(rest_kernel, (bf16(ANS_LEN, group), bf16(ANS_LEN, group), bf16(ANS_L...  4.16 us
    ppermute x1, starting transfers between devices, body(): sibling = lax.ppermute(own, 'c', OTHER_CORE)  2.43 us
    pallas_call x1, Pallas kernels, body(): call(own_kernel, (vmem(ROWS, HEAD_DIM), vmem(ROWS, HEAD_DIM), vmem(24, AN...  1.96 us
    pallas_call x1, Pallas kernels, body(): call(far_kernel, (vmem(HALF, 2 * HEAD_DIM), vmem(PROMPT, ALL), vmem(PROMP...  1.86 us
  transfers between devices with their start and end apart: 4, of which 4 were waited for; matrix products, arithmetic and copies ran while one was open for 0% of the time, Pallas kernels for 13%

profile of v2, /device:TPU:1, one launch (start us, length us, event | category | flops | bytes accessed | tf_op | source)
XLA Modules:
  0.0 58.3 jit_solution(1525949658425723651)
XLA Ops:
  0.6 1.6 %shard_map.161 = bf16[128,2,384]{2,1,0:T(2,128)(2,1)} custom-call(bf16[2,5120]{1,0:T(2,128)(2,1)} %q_hbm.1, bf16[2,5120]{1,0:T(2,128)(2,1)} %g_hbm.1, bf16[2,1024]{1,0:T(2,128)(2,1)} %k_hbm.1, bf16[2,1024]{1,0:T(2,128)(2,1)} %v_hbm.1), custom_call_target="tpu_custom_call" | custom-call | tf_op jit(solution)/shard_map/pallas_call | solution.py:341
  2.2 16.3 %all-to-all-start = ((bf16[128,2,384]{2,1,0:T(2,128)(2,1)}), bf16[128,2,384]{2,1,0:T(2,128)(2,1)S(1)}, u32[]{:S(2)}, u32[]{:S(2)}) async-start(bf16[128,2,384]{2,1,0:T(2,128)(2,1)} %shard_map.161), calls=%async_computation | async-start | bytes 393216 | tf_op jit(solution)/shard_map/all_to_all | solution.py:353
  19.2 2.0 %shard_map.162 = (bf16[1280,128]{1,0:T(8,128)(2,1)S(1)}, bf16[1280,128]{1,0:T(8,128)(2,1)S(1)}, f32[24,256]{1,0:T(8,128)S(1)}, f32[512,128]{1,0:T(8,128)S(1)}) custom-call(s32[1]{0:T(128)S(6)} %copy.18.len_ref, s32[1,512]{1,0:T(1,128)} %bitcast.21, bf16[256,640]{1,0:T(8,128)(2,1)} %bitcast.9, bf16[256,128]{1,0:T(8,128)(2,1)} %bitcast.13, ...), custom_call_target="tpu_custom_call" | custom-call | flops 400000000 | bytes 2000000 | tf_op jit(solution)/shard_map/pallas_call | solution.py:356
  21.2 9.6 %all-to-all-done = bf16[128,2,384]{2,1,0:T(2,128)(2,1)S(1)} async-done(((bf16[128,2,384]{2,1,0:T(2,128)(2,1)}), bf16[128,2,384]{2,1,0:T(2,128)(2,1)S(1)}, u32[]{:S(2)}, u32[]{:S(2)}) %all-to-all-start) | async-done | bytes 196640 | tf_op jit(solution)/shard_map/all_to_all | solution.py:353
  30.9 0.1 reshape.22.own_ref
  30.9 2.4 %collective-permute-start = (bf16[256,384]{1,0:T(8,128)(2,1)S(1)}, bf16[256,384]{1,0:T(8,128)(2,1)S(1)}, u32[]{:S(2)}, u32[]{:S(2)}) collective-permute-start(bf16[256,384]{1,0:T(8,128)(2,1)S(1)} %reshape.22.own_ref), channel_id=1, source_target_pairs={{0,8},{8,0},{1,9},{9,1},{2,10},{10,2},{3,11},{11,3},{4,12},{12,4},... | collective-permute-start | bytes 589832 | tf_op jit(solution)/shard_map/ppermute | solution.py:374
  33.4 0.7 %shard_map.163 = (f32[256,1408]{1,0:T(8,128)S(1)}, f32[256,128]{1,0:T(8,128)S(1)}, bf16[256,128]{1,0:T(8,128)(2,1)S(1)}, f32[24,256]{1,0:T(8,128)S(1)}, bf16[128...) custom-call(f32[512,128]{1,0:T(8,128)S(1)} %get-tuple-element.42.bias_ref, bf16[256,384]{1,0:T(8,128)(2,1)S(1)} %reshape.22.own_ref, ...), custom_call_target="tpu_custom_call" | custom-call | flops 200000000 | bytes 2000000 | tf_op jit(solution)/shard_map/pallas_call | solution.py:375
  34.1 0.3 collective-permute-done.sib_ref
  34.4 1.9 %shard_map.164 = (bf16[256,256]{1,0:T(8,128)(2,1)S(1)}, bf16[512,1408]{1,0:T(8,128)(2,1)S(1)}, bf16[512,1408]{1,0:T(8,128)(2,1)S(1)}, f32[16,256]{1,0:T(8,128)S(1)}) custom-call(f32[256,128]{1,0:T(8,128)S(1)} %get-tuple-element.49.bias_ref, bf16[256,384]{1,0:T(8,128)(2,1)S(1)} %reshape.22.own_ref, bf16[256,384]{1,0:T(8,128)(2,1)S(1)} %collective-permute-done.sib_ref, ...), custom_call_target="tpu_custom_call" | custom-call | flops 400000000 | bytes 2000000 | tf_op jit(solution)/shard_map/pallas_call | solution.py:384
  36.3 0.5 collective-permute-start.1
  36.8 0.9 %shard_map.165 = (f32[256,256]{1,0:T(8,128)S(1)}, bf16[256,128]{1,0:T(8,128)(2,1)S(1)}) custom-call(bf16[256,384]{1,0:T(8,128)(2,1)S(1)} %reshape.22.own_ref, bf16[256,384]{1,0:T(8,128)(2,1)S(1)} %collective-permute-done.sib_ref, bf16[1280,128]{1,0:T(8,128)(2,1)S(1)} %get-tuple-element.46.q_ref, bf16[1280,128]{1,0:T(8,128)(2,1)S(1)} %get-tuple-element.47.g_ref, ...), custom_call_target="tpu_custom_call" | custom-call | flops 200000000 | bytes 2000000 | tf_op jit(solution)/shard_map/pallas_call | solution.py:395
  37.6 0.1 collective-permute-done.1.other_ref
  37.7 0.1 shard_map.166
  37.8 0.0 copy-start
  37.9 0.7 %copy-done = bf16[128,2,384]{2,1,0:T(2,128)(2,1)} copy-done((bf16[128,2,384]{2,1,0:T(2,128)(2,1)}, bf16[128,2,384]{2,1,0:T(2,128)(2,1)S(1)}, u32[]{:S(2)}) %copy-start) | copy-done | bytes 196632
  38.5 6.1 %all-to-all-start.1 = ((bf16[128,2,384]{2,1,0:T(2,128)(2,1)}), bf16[128,2,384]{2,1,0:T(2,128)(2,1)S(1)}, u32[]{:S(2)}, u32[]{:S(2)}) async-start(bf16[128,2,384]{2,1,0:T(2,128)(2,1)} %copy-done), calls=%async_computation.1 | async-start | bytes 393216 | tf_op jit(solution)/shard_map/all_to_all | solution.py:405
  44.7 4.2 %shard_map.168 = (bf16[256,640]{1,0:T(8,128)(2,1)}, bf16[256,640]{1,0:T(8,128)(2,1)}, bf16[256,128]{1,0:T(8,128)(2,1)}, bf16[256,128]{1,0:T(8,128)(2,1)}) custom-call(s32[1]{0:T(128)S(6)} %copy.18.len_ref, bf16[256,640]{1,0:T(8,128)(2,1)} %bitcast.10, bf16[256,128]{1,0:T(8,128)(2,1)} %bitcast.14, bf16[256,128]{1,0:T(8,128)(2,1)} %bitcast.16, ...), custom_call_target="tpu_custom_call" | custom-call | flops 700000000 | bytes 2000000 | tf_op jit(solution)/shard_map/pallas_call | solution.py:406
  48.9 8.7 %all-to-all-done.1.x_ref = bf16[128,2,384]{2,1,0:T(2,128)(2,1)S(1)} async-done(((bf16[128,2,384]{2,1,0:T(2,128)(2,1)}), bf16[128,2,384]{2,1,0:T(2,128)(2,1)S(1)}, u32[]{:S(2)}, u32[]{:S(2)}) %all-to-all-start.1) | async-done | bytes 196640 | tf_op jit(solution)/shard_map/all_to_all | solution.py:405
  57.5 0.7 %shard_map.167 = (bf16[2,5120]{1,0:T(2,128)(2,1)}, bf16[2,5120]{1,0:T(2,128)(2,1)}, bf16[2,1024]{1,0:T(2,128)(2,1)}, bf16[2,1024]{1,0:T(2,128)(2,1)}) custom-call(bf16[128,2,384]{2,1,0:T(2,128)(2,1)S(1)} %all-to-all-done.1.x_ref), custom_call_target="tpu_custom_call" | custom-call | tf_op jit(solution)/shard_map/pallas_call | solution.py:423
Async XLA Ops:
  2.2 28.6 %all-to-all-start = ((bf16[128,2,384]{2,1,0:T(2,128)(2,1)}), bf16[128,2,384]{2,1,0:T(2,128)(2,1)S(1)}, u32[]{:S(2)}, u32[]{:S(2)}) async-start(bf16[128,2,384]{2,1,0:T(2,128)(2,1)} %shard_map.161), calls=%async_computation | async-start | bytes 393216 | tf_op jit(solution)/shard_map/all_to_all | solution.py:353
  30.9 3.5 %collective-permute-start = (bf16[256,384]{1,0:T(8,128)(2,1)S(1)}, bf16[256,384]{1,0:T(8,128)(2,1)S(1)}, u32[]{:S(2)}, u32[]{:S(2)}) collective-permute-start(bf16[256,384]{1,0:T(8,128)(2,1)S(1)} %reshape.22.own_ref), channel_id=1, source_target_pairs={{0,8},{8,0},{1,9},{9,1},{2,10},{10,2},{3,11},{11,3},{4,12},{12,4},... | collective-permute-start | bytes 589832 | tf_op jit(solution)/shard_map/ppermute | solution.py:374
  36.3 1.4 %collective-permute-start.1 = (bf16[256,256]{1,0:T(8,128)(2,1)S(1)}, bf16[256,256]{1,0:T(8,128)(2,1)S(1)}, u32[]{:S(2)}, u32[]{:S(2)}) collective-permute-start(bf16[256,256]{1,0:T(8,128)(2,1)S(1)} %get-tuple-element.55), channel_id=1, source_target_pairs={{0,8},{8,0},{1,9},{9,1},{2,10},{10,2},{3,11},{11,3},{4,12},{12,4},... | collective-permute-start | bytes 393224 | tf_op jit(solution)/shard_map/ppermute | solution.py:394
  37.8 0.7 %copy-start = (bf16[128,2,384]{2,1,0:T(2,128)(2,1)}, bf16[128,2,384]{2,1,0:T(2,128)(2,1)S(1)}, u32[]{:S(2)}) copy-start(bf16[128,2,384]{2,1,0:T(2,128)(2,1)S(1)} %shard_map.166) | copy-start | bytes 589828
  38.5 19.0 %all-to-all-start.1 = ((bf16[128,2,384]{2,1,0:T(2,128)(2,1)}), bf16[128,2,384]{2,1,0:T(2,128)(2,1)S(1)}, u32[]{:S(2)}, u32[]{:S(2)}) async-start(bf16[128,2,384]{2,1,0:T(2,128)(2,1)} %copy-done), calls=%async_computation.1 | async-start | bytes 393216 | tf_op jit(solution)/shard_map/all_to_all | solution.py:405

commit v3 on v2

--- a/solution.py
+++ b/solution.py
@@ -24,7 +24,8 @@
 SCALE2 = SCALING / math.log(2.0)
 SEQ_AXES = ("y", "zh", "c")
 HEAD_AXES = ("x", "zl")
-SAME_CORE = ("y", "zh", "x", "zl")
+PEER_BITS = ("z0", "x1", "x0", "z2", "z1", "y1", "y0")
+PEER_FLIP = 106
 OTHER_CORE = [(0, 1), (1, 0)]
 VMEM = pl.BlockSpec(memory_space=pltpu.VMEM)
 SMEM = pl.BlockSpec(memory_space=pltpu.SMEM)
@@ -45,6 +46,33 @@
 
 def head(n):
     return slice(n * ANS_LEN, min((n + 1) * ANS_LEN, ALL))
+
+
+def number(peer, names):
+    total = 0
+    for name in names:
+        place = 6 - PEER_BITS.index(name)
+        total = total * 2 + (((peer >> place) & 1) ^ ((PEER_FLIP >> place) & 1))
+    return total
+
+
+def group_of(peer):
+    return number(peer, ("x1", "x0", "z0"))
+
+
+def place_of(peer):
+    return number(peer, ("y1", "y0", "z2", "z1"))
+
+
+def row_at(peer, side, row):
+    return (place_of(peer) * 2 + side) * 16 + group_of(peer) * 2 + row
+
+
+def peer_groups():
+    return [
+        [place_of(peer) * 16 + core * 8 + group_of(peer) for peer in range(SENDERS)]
+        for core in range(2)
+    ]
 
 
 def pack_kernel(q_hbm, g_hbm, k_hbm, v_hbm, o_ref, q_ref, g_ref, k_ref, v_ref, sems):
@@ -58,29 +86,29 @@
     g = g_ref[...].astype(F32)
     zero = jnp.zeros((2, HEAD_DIM), BF16)
     rows = [jnp.concatenate([q[r : r + 1], g[r : r + 1]], axis=0).astype(BF16) for r in range(2)]
-    for h in range(KV_HEADS):
-        k = k_ref[:, cols(h)]
-        v = v_ref[:, cols(h)]
-        for yz in range(PEERS):
-            o_ref[yz * KV_HEADS + h, :, cols(0)] = k
-            o_ref[yz * KV_HEADS + h, :, cols(1)] = v
-            if yz < PAIRS:
-                pair = rows[yz // GROUP][:, cols(h * GROUP + yz % GROUP)]
-            else:
-                pair = zero
-            o_ref[yz * KV_HEADS + h, :, cols(2)] = pair
+    for peer in range(SENDERS):
+        h = group_of(peer)
+        d = place_of(peer)
+        o_ref[peer, :, cols(0)] = k_ref[:, cols(h)]
+        o_ref[peer, :, cols(1)] = v_ref[:, cols(h)]
+        if d < PAIRS:
+            pair = rows[d // GROUP][:, cols(h * GROUP + d % GROUP)]
+        else:
+            pair = zero
+        o_ref[peer, :, cols(2)] = pair
 
 
 def unpack_kernel(x_ref, out_ref, dq_ref, dk_ref, dv_ref):
+    peer_at = {(group_of(peer), place_of(peer)): peer for peer in range(SENDERS)}
     for h in range(KV_HEADS):
         total = jnp.zeros((2, 2 * HEAD_DIM), F32)
-        for yz in range(PEERS):
-            total += x_ref[yz * KV_HEADS + h, :, : 2 * HEAD_DIM].astype(F32)
+        for d in range(PEERS):
+            total += x_ref[peer_at[h, d], :, : 2 * HEAD_DIM].astype(F32)
         dk_ref[:, cols(h)] = total[:, :HEAD_DIM].astype(BF16)
         dv_ref[:, cols(h)] = total[:, HEAD_DIM:].astype(BF16)
         for n in range(GROUP):
-            first = x_ref[n * KV_HEADS + h, :, cols(2)].astype(F32)
-            second = x_ref[(GROUP + n) * KV_HEADS + h, :, cols(2)].astype(F32)
+            first = x_ref[peer_at[h, n], :, cols(2)].astype(F32)
+            second = x_ref[peer_at[h, GROUP + n], :, cols(2)].astype(F32)
             at = cols(h * GROUP + n)
             out_ref[:, at] = jnp.concatenate([first[:1], second[:1]], axis=0).astype(BF16)
             dq_ref[:, at] = jnp.concatenate([first[1:], second[1:]], axis=0).astype(BF16)
@@ -135,15 +163,13 @@
     core = lax.axis_index("c")
     row = jnp.where(lax.axis_index("y") * 4 + lax.axis_index("zh") >= GROUP, 1, 0)
 
-    shape = (PROMPT, PROMPT)
-    j = lax.broadcasted_iota(jnp.int32, shape, 0)
+    j = lax.broadcasted_iota(jnp.int32, (PROMPT, 1), 0)
     side = jnp.where(j < HALF, core, 1 - core)
-    at = ((j & (HALF - 1)) >> 4) * 32 + side * 16 + (j & 15)
-    key_pick = (at == lax.broadcasted_iota(jnp.int32, shape, 1)).astype(BF16)
-    shape = (SENDERS, PROMPT)
-    i = lax.broadcasted_iota(jnp.int32, shape, 0)
-    at = (i >> 3) * 32 + core * 16 + (i & 7) * 2 + row
-    row_pick = (at == lax.broadcasted_iota(jnp.int32, shape, 1)).astype(BF16)
+    at = row_at((j & (HALF - 1)) >> 1, side, j & 1)
+    key_pick = (at == lax.broadcasted_iota(jnp.int32, (PROMPT, PROMPT), 1)).astype(BF16)
+    i = lax.broadcasted_iota(jnp.int32, (SENDERS, 1), 0)
+    at = row_at(i, core, row)
+    row_pick = (at == lax.broadcasted_iota(jnp.int32, (SENDERS, PROMPT), 1)).astype(BF16)
     copies[0].wait()
     segments = jnp.broadcast_to(seg_ref[...].astype(F32), (SENDERS, PROMPT)).astype(BF16)
     key_segments = dot(key_pick, segments, NT)
@@ -331,6 +357,13 @@
     return pltpu.with_memory_space_constraint(x, pltpu.VMEM)
 
 
+def exchange(x):
+    return lax.all_to_all(
+        x, SEQ_AXES + HEAD_AXES, split_axis=0, concat_axis=0, tiled=True,
+        axis_index_groups=peer_groups(),
+    )
+
+
 def body(
     prompt_q, prompt_k, prompt_v, prompt_grad, segment_ids,
     answer_q, answer_k, answer_v, answer_grad, answer_lengths,
@@ -350,7 +383,7 @@
         limit=4,
     )(in_hbm(prompt_q), in_hbm(prompt_grad), in_hbm(prompt_k), in_hbm(prompt_v))
     packed, answer_q = lax.optimization_barrier((packed, answer_q))
-    own = lax.all_to_all(packed, SAME_CORE, split_axis=0, concat_axis=0, tiled=True)
+    own = exchange(packed)
     own = own.reshape(HALF, 3 * HEAD_DIM)
 
     queries, grads, stat, bias = call(
@@ -402,7 +435,7 @@
         post_kernel, bf16(SENDERS, 2, 3 * HEAD_DIM), [VMEM] * 3, limit=4, moved=700_000
     )(d_own, d_mine, pair)
     back, stat = lax.optimization_barrier((back, stat))
-    back = lax.all_to_all(back, SAME_CORE, split_axis=0, concat_axis=0, tiled=True)
+    back = exchange(back)
     a_out, a_dq, a_dk, a_dv = call(
         rest_kernel,
         (

time: 58.6 us -> 51.1 us (0.87)
  waiting for transfers between devices: 18.8 us -> 2.46 us
  starting transfers between devices: 25.4 us -> 34.2 us
    all_to_all x2, waiting for transfers between devices: 18.3 us -> 2.02 us  [exchange(): lax.all_to_all(x, SEQ_AXES + HEAD_AXES, split_axis=0, concat_axis=0, tile...]
    all_to_all x2, starting transfers between devices: 22.5 us -> 32.1 us  [exchange(): lax.all_to_all(x, SEQ_AXES + HEAD_AXES, split_axis=0, concat_axis=0, tile...]
    ppermute x1, starting transfers between devices: 2.43 us -> 1.63 us  [body(): sibling = lax.ppermute(own, 'c', OTHER_CORE)]
  transfers between devices with their start and end apart: 4 -> 4, of which waited for: 4 -> 4; matrix products, arithmetic and copies ran while one was open for 0% -> 0% of each run, Pallas kernels for 13% -> 15%
where the time goes in v3:
time: 51.1 us; the launch traced here: 50.7 us
  starting transfers between devices  34.2 us (67%)
  Pallas kernels  12 us (23%)
  waiting for transfers between devices  2.46 us (5%)
  between operations  1.35 us (3%)
  local copies, waits for them, and re-layouts  0.75 us (1%)
    all_to_all x2, starting transfers between devices, exchange(): lax.all_to_all(x, SEQ_AXES + HEAD_AXES, split_axis=0, concat_axis=0, tile...  32.1 us
    pallas_call x1, Pallas kernels, body(): call(rest_kernel, (bf16(ANS_LEN, group), bf16(ANS_LEN, group), bf16(ANS_L...  4.17 us
    all_to_all x2, waiting for transfers between devices, exchange(): lax.all_to_all(x, SEQ_AXES + HEAD_AXES, split_axis=0, concat_axis=0, tile...  2.02 us
    pallas_call x1, Pallas kernels, body(): call(own_kernel, (vmem(ROWS, HEAD_DIM), vmem(ROWS, HEAD_DIM), vmem(24, AN...  1.96 us
    pallas_call x1, Pallas kernels, body(): call(far_kernel, (vmem(HALF, 2 * HEAD_DIM), vmem(PROMPT, ALL), vmem(PROMP...  1.86 us
    ppermute x1, starting transfers between devices, body(): sibling = lax.ppermute(own, 'c', OTHER_CORE)  1.63 us
    pallas_call x1, Pallas kernels, body(): call(pack_kernel, bf16(SENDERS, 2, 3 * HEAD_DIM), [HBM] * 4, scratch=[plt...  1.6 us
  transfers between devices with their start and end apart: 4, of which 4 were waited for; matrix products, arithmetic and copies ran while one was open for 0% of the time, Pallas kernels for 15%

profile of v3, /device:TPU:1, one launch (start us, length us, event | category | flops | bytes accessed | tf_op | source)
XLA Modules:
  0.0 50.7 jit_solution(9485825775438691523)
XLA Ops:
  0.6 1.6 %shard_map.161 = bf16[128,2,384]{2,1,0:T(2,128)(2,1)} custom-call(bf16[2,5120]{1,0:T(2,128)(2,1)} %q_hbm.1, bf16[2,5120]{1,0:T(2,128)(2,1)} %g_hbm.1, bf16[2,1024]{1,0:T(2,128)(2,1)} %k_hbm.1, bf16[2,1024]{1,0:T(2,128)(2,1)} %v_hbm.1), custom_call_target="tpu_custom_call" | custom-call | tf_op jit(solution)/shard_map/pallas_call | solution.py:374
  2.2 18.3 %all-to-all-start = ((bf16[128,2,384]{2,1,0:T(2,128)(2,1)}), bf16[128,2,384]{2,1,0:T(2,128)(2,1)S(1)}, u32[]{:S(2)}, u32[]{:S(2)}) async-start(bf16[128,2,384]{2,1,0:T(2,128)(2,1)} %shard_map.161), calls=%async_computation | async-start | bytes 393216 | tf_op jit(solution)/shard_map/all_to_all | solution.py:361
  21.2 2.0 %shard_map.162 = (bf16[1280,128]{1,0:T(8,128)(2,1)S(1)}, bf16[1280,128]{1,0:T(8,128)(2,1)S(1)}, f32[24,256]{1,0:T(8,128)S(1)}, f32[512,128]{1,0:T(8,128)S(1)}) custom-call(s32[1]{0:T(128)S(6)} %copy.18.len_ref, s32[1,512]{1,0:T(1,128)} %bitcast.21, bf16[256,640]{1,0:T(8,128)(2,1)} %bitcast.9, bf16[256,128]{1,0:T(8,128)(2,1)} %bitcast.13, ...), custom_call_target="tpu_custom_call" | custom-call | flops 400000000 | bytes 2000000 | tf_op jit(solution)/shard_map/pallas_call | solution.py:389
  23.1 1.7 %all-to-all-done = bf16[128,2,384]{2,1,0:T(2,128)(2,1)S(1)} async-done(((bf16[128,2,384]{2,1,0:T(2,128)(2,1)}), bf16[128,2,384]{2,1,0:T(2,128)(2,1)S(1)}, u32[]{:S(2)}, u32[]{:S(2)}) %all-to-all-start) | async-done | bytes 196640 | tf_op jit(solution)/shard_map/all_to_all | solution.py:361
  24.9 0.1 reshape.22.own_ref
  24.9 1.6 %collective-permute-start = (bf16[256,384]{1,0:T(8,128)(2,1)S(1)}, bf16[256,384]{1,0:T(8,128)(2,1)S(1)}, u32[]{:S(2)}, u32[]{:S(2)}) collective-permute-start(bf16[256,384]{1,0:T(8,128)(2,1)S(1)} %reshape.22.own_ref), channel_id=1, source_target_pairs={{0,8},{8,0},{1,9},{9,1},{2,10},{10,2},{3,11},{11,3},{4,12},{12,4},... | collective-permute-start | bytes 589832 | tf_op jit(solution)/shard_map/ppermute | solution.py:407
  26.6 0.7 %shard_map.163 = (f32[256,1408]{1,0:T(8,128)S(1)}, f32[256,128]{1,0:T(8,128)S(1)}, bf16[256,128]{1,0:T(8,128)(2,1)S(1)}, f32[24,256]{1,0:T(8,128)S(1)}, bf16[128...) custom-call(f32[512,128]{1,0:T(8,128)S(1)} %get-tuple-element.42.bias_ref, bf16[256,384]{1,0:T(8,128)(2,1)S(1)} %reshape.22.own_ref, ...), custom_call_target="tpu_custom_call" | custom-call | flops 200000000 | bytes 2000000 | tf_op jit(solution)/shard_map/pallas_call | solution.py:408
  27.3 0.4 collective-permute-done.sib_ref
  27.6 1.9 %shard_map.164 = (bf16[256,256]{1,0:T(8,128)(2,1)S(1)}, bf16[512,1408]{1,0:T(8,128)(2,1)S(1)}, bf16[512,1408]{1,0:T(8,128)(2,1)S(1)}, f32[16,256]{1,0:T(8,128)S(1)}) custom-call(f32[256,128]{1,0:T(8,128)S(1)} %get-tuple-element.49.bias_ref, bf16[256,384]{1,0:T(8,128)(2,1)S(1)} %reshape.22.own_ref, bf16[256,384]{1,0:T(8,128)(2,1)S(1)} %collective-permute-done.sib_ref, ...), custom_call_target="tpu_custom_call" | custom-call | flops 400000000 | bytes 2000000 | tf_op jit(solution)/shard_map/pallas_call | solution.py:417
  29.5 0.5 collective-permute-start.1
  30.0 0.9 %shard_map.165 = (f32[256,256]{1,0:T(8,128)S(1)}, bf16[256,128]{1,0:T(8,128)(2,1)S(1)}) custom-call(bf16[256,384]{1,0:T(8,128)(2,1)S(1)} %reshape.22.own_ref, bf16[256,384]{1,0:T(8,128)(2,1)S(1)} %collective-permute-done.sib_ref, bf16[1280,128]{1,0:T(8,128)(2,1)S(1)} %get-tuple-element.46.q_ref, bf16[1280,128]{1,0:T(8,128)(2,1)S(1)} %get-tuple-element.47.g_ref, ...), custom_call_target="tpu_custom_call" | custom-call | flops 200000000 | bytes 2000000 | tf_op jit(solution)/shard_map/pallas_call | solution.py:428
  30.9 0.1 collective-permute-done.1.other_ref
  31.0 0.1 shard_map.166
  31.1 0.0 copy-start
  31.1 0.7 %copy-done = bf16[128,2,384]{2,1,0:T(2,128)(2,1)} copy-done((bf16[128,2,384]{2,1,0:T(2,128)(2,1)}, bf16[128,2,384]{2,1,0:T(2,128)(2,1)S(1)}, u32[]{:S(2)}) %copy-start) | copy-done | bytes 196632
  31.7 13.8 %all-to-all-start.1 = ((bf16[128,2,384]{2,1,0:T(2,128)(2,1)}), bf16[128,2,384]{2,1,0:T(2,128)(2,1)S(1)}, u32[]{:S(2)}, u32[]{:S(2)}) async-start(bf16[128,2,384]{2,1,0:T(2,128)(2,1)} %copy-done), calls=%async_computation.1 | async-start | bytes 393216 | tf_op jit(solution)/shard_map/all_to_all | solution.py:361
  45.5 4.2 %shard_map.168 = (bf16[256,640]{1,0:T(8,128)(2,1)}, bf16[256,640]{1,0:T(8,128)(2,1)}, bf16[256,128]{1,0:T(8,128)(2,1)}, bf16[256,128]{1,0:T(8,128)(2,1)}) custom-call(s32[1]{0:T(128)S(6)} %copy.18.len_ref, bf16[256,640]{1,0:T(8,128)(2,1)} %bitcast.10, bf16[256,128]{1,0:T(8,128)(2,1)} %bitcast.14, bf16[256,128]{1,0:T(8,128)(2,1)} %bitcast.16, ...), custom_call_target="tpu_custom_call" | custom-call | flops 700000000 | bytes 2000000 | tf_op jit(solution)/shard_map/pallas_call | solution.py:439
  49.7 0.3 all-to-all-done.1.x_ref
  50.0 0.7 %shard_map.167 = (bf16[2,5120]{1,0:T(2,128)(2,1)}, bf16[2,5120]{1,0:T(2,128)(2,1)}, bf16[2,1024]{1,0:T(2,128)(2,1)}, bf16[2,1024]{1,0:T(2,128)(2,1)}) custom-call(bf16[128,2,384]{2,1,0:T(2,128)(2,1)S(1)} %all-to-all-done.1.x_ref), custom_call_target="tpu_custom_call" | custom-call | tf_op jit(solution)/shard_map/pallas_call | solution.py:456
Async XLA Ops:
  2.2 22.6 %all-to-all-start = ((bf16[128,2,384]{2,1,0:T(2,128)(2,1)}), bf16[128,2,384]{2,1,0:T(2,128)(2,1)S(1)}, u32[]{:S(2)}, u32[]{:S(2)}) async-start(bf16[128,2,384]{2,1,0:T(2,128)(2,1)} %shard_map.161), calls=%async_computation | async-start | bytes 393216 | tf_op jit(solution)/shard_map/all_to_all | solution.py:361
  24.9 2.7 %collective-permute-start = (bf16[256,384]{1,0:T(8,128)(2,1)S(1)}, bf16[256,384]{1,0:T(8,128)(2,1)S(1)}, u32[]{:S(2)}, u32[]{:S(2)}) collective-permute-start(bf16[256,384]{1,0:T(8,128)(2,1)S(1)} %reshape.22.own_ref), channel_id=1, source_target_pairs={{0,8},{8,0},{1,9},{9,1},{2,10},{10,2},{3,11},{11,3},{4,12},{12,4},... | collective-permute-start | bytes 589832 | tf_op jit(solution)/shard_map/ppermute | solution.py:407
  29.5 1.4 %collective-permute-start.1 = (bf16[256,256]{1,0:T(8,128)(2,1)S(1)}, bf16[256,256]{1,0:T(8,128)(2,1)S(1)}, u32[]{:S(2)}, u32[]{:S(2)}) collective-permute-start(bf16[256,256]{1,0:T(8,128)(2,1)S(1)} %get-tuple-element.55), channel_id=1, source_target_pairs={{0,8},{8,0},{1,9},{9,1},{2,10},{10,2},{3,11},{11,3},{4,12},{12,4},... | collective-permute-start | bytes 393224 | tf_op jit(solution)/shard_map/ppermute | solution.py:427
  31.1 0.7 %copy-start = (bf16[128,2,384]{2,1,0:T(2,128)(2,1)}, bf16[128,2,384]{2,1,0:T(2,128)(2,1)S(1)}, u32[]{:S(2)}) copy-start(bf16[128,2,384]{2,1,0:T(2,128)(2,1)S(1)} %shard_map.166) | copy-start | bytes 589828
  31.7 18.3 %all-to-all-start.1 = ((bf16[128,2,384]{2,1,0:T(2,128)(2,1)}), bf16[128,2,384]{2,1,0:T(2,128)(2,1)S(1)}, u32[]{:S(2)}, u32[]{:S(2)}) async-start(bf16[128,2,384]{2,1,0:T(2,128)(2,1)} %copy-done), calls=%async_computation.1 | async-start | bytes 393216 | tf_op jit(solution)/shard_map/all_to_all | solution.py:361

commit v4 on v3

--- a/solution.py
+++ b/solution.py
@@ -189,125 +189,114 @@
         scores = jnp.where(seen, dot(keys, q_ref[head(n)], NT), NEG)
         top = column_max(scores)
         weights = jnp.exp2(scores * SCALE2 - top * SCALE2)
-        stat_ref[n : n + 1] = top
-        stat_ref[8 + n : 9 + n] = column_sum(weights)
-        stat_ref[16 + n : 17 + n] = column_sum(weights * dot(values, grads, NT))
+        stat_ref[0:1, head(n)] = top
+        stat_ref[1:2, head(n)] = column_sum(weights)
+        stat_ref[2:3, head(n)] = column_sum(weights * dot(values, grads, NT))
 
 
 def near_kernel(
     bias_ref, own_ref, q_ref, g_ref, stat_ref,
-    e_ref, far_bias_ref, moved_ref, stat2_ref, q2_ref, g2_ref,
+    e_ref, far_bias_ref, stat2_ref, q2_ref, g2_ref,
 ):
     keys = own_ref[:, cols(0)]
     values = own_ref[:, cols(1)]
-    moved_ref[...] = dot(deinterleave(0), own_ref[:, cols(2)], NN).astype(BF16)
+    moved = dot(deinterleave(0), own_ref[:, cols(2)], NN).astype(BF16)
     far_bias_ref[...] = bias_ref[HALF:]
-    q2_ref[...] = q_ref[...]
-    g2_ref[...] = g_ref[...]
+    q2_ref[:ROWS] = q_ref[...]
+    g2_ref[:ROWS] = g_ref[...]
+    q2_ref[ROWS:] = moved[:SENDERS]
+    g2_ref[ROWS:] = moved[SENDERS:]
     for n in range(GROUP + 1):
         if n < GROUP:
             scores = dot(keys, q_ref[head(n)], NT)
             prob_grad = dot(values, g_ref[head(n)], NT)
-            old_top = stat_ref[n : n + 1]
+            old_top = stat_ref[0:1, head(n)]
             top = jnp.maximum(column_max(scores), old_top)
         else:
-            scores = dot(keys, moved_ref[:SENDERS], NT) + bias_ref[:HALF]
-            prob_grad = dot(values, moved_ref[SENDERS:], NT)
+            scores = dot(keys, moved[:SENDERS], NT) + bias_ref[:HALF]
+            prob_grad = dot(values, moved[SENDERS:], NT)
             top = column_max(scores)
         weights = jnp.exp2(scores * SCALE2 - top * SCALE2)
         total = column_sum(weights)
         moment = column_sum(weights * prob_grad)
         if n < GROUP:
             shift = jnp.exp2((old_top - top) * SCALE2)
-            total += stat_ref[8 + n : 9 + n] * shift
-            moment += stat_ref[16 + n : 17 + n] * shift
+            total += stat_ref[1:2, head(n)] * shift
+            moment += stat_ref[2:3, head(n)] * shift
         e_ref[:, head(n)] = weights
-        wide = slice(0, weights.shape[1])
-        stat2_ref[n : n + 1, wide] = top
-        stat2_ref[8 + n : 9 + n, wide] = total
-        stat2_ref[16 + n : 17 + n, wide] = moment
+        stat2_ref[0:1, head(n)] = top
+        stat2_ref[1:2, head(n)] = total
+        stat2_ref[2:3, head(n)] = moment
 
 
 def far_kernel(
-    bias_ref, own_ref, sib_ref, q_ref, g_ref, e_ref, moved_ref, stat_ref,
-    dsib_ref, w_ref, ds_ref, stat2_ref,
-):
-    keys = sib_ref[:, cols(0)]
-    values = sib_ref[:, cols(1)]
-    near_values = own_ref[:, cols(1)]
-    for n in range(GROUP + 1):
-        if n < GROUP:
-            scores = dot(keys, q_ref[head(n)], NT)
-            grads = g_ref[head(n)]
-        else:
-            scores = dot(keys, moved_ref[:SENDERS], NT) + bias_ref[...]
-            grads = moved_ref[SENDERS:]
-        prob_grad = dot(values, grads, NT)
-        wide = slice(0, scores.shape[1])
-        old_top = stat_ref[n : n + 1, wide]
-        top = jnp.maximum(column_max(scores), old_top)
-        shift = jnp.exp2((old_top - top) * SCALE2)
-        weights = jnp.exp2(scores * SCALE2 - top * SCALE2)
-        total = column_sum(weights) + stat_ref[8 + n : 9 + n, wide] * shift
-        moment = column_sum(weights * prob_grad) + stat_ref[16 + n : 17 + n, wide] * shift
-        inverse = 1.0 / total
-        delta = moment * inverse
-        if n < GROUP:
-            stat2_ref[n : n + 1] = top * SCALE2 + jnp.log2(total)
-            stat2_ref[8 + n : 9 + n] = delta
-        weights = weights * inverse
-        w_ref[HALF:, head(n)] = weights.astype(BF16)
-        ds_ref[HALF:, head(n)] = (weights * (prob_grad - delta)).astype(BF16)
-        weights = e_ref[:, head(n)] * (shift * inverse)
-        w_ref[:HALF, head(n)] = weights.astype(BF16)
-        ds_ref[:HALF, head(n)] = (weights * (dot(near_values, grads, NT) - delta)).astype(BF16)
-    dk, dv = key_terms(ds_ref[HALF:], w_ref[HALF:], q_ref, g_ref, moved_ref)
-    dsib_ref[:, cols(0)] = dk.astype(BF16)
-    dsib_ref[:, cols(1)] = dv.astype(BF16)
-
-
-def key_terms(score_grad, weights, q_ref, g_ref, moved_ref):
-    dk = dot(score_grad[:, :ROWS], q_ref[...], NN)
-    dk += dot(score_grad[:, ROWS:], moved_ref[:SENDERS], NN)
-    dv = dot(weights[:, :ROWS], g_ref[...], NN)
-    dv += dot(weights[:, ROWS:], moved_ref[SENDERS:], NN)
-    return dk * SCALING, dv
+    bias_ref, sib_ref, q_ref, g_ref, stat_ref, dsib_ref, w_ref, ds_ref, stat2_ref
+):
+    scores = dot(sib_ref[:, cols(0)], q_ref[...], NT)
+    scores = jnp.concatenate([scores[:, :ROWS], scores[:, ROWS:] + bias_ref[...]], axis=1)
+    prob_grad = dot(sib_ref[:, cols(1)], g_ref[...], NT)
+    old_top = stat_ref[0:1]
+    top = jnp.maximum(column_max(scores), old_top)
+    shift = jnp.exp2((old_top - top) * SCALE2)
+    weights = jnp.exp2(scores * SCALE2 - top * SCALE2)
+    total = column_sum(weights) + stat_ref[1:2] * shift
+    moment = column_sum(weights * prob_grad) + stat_ref[2:3] * shift
+    inverse = 1.0 / total
+    delta = moment * inverse
+    stat2_ref[0:1] = top * SCALE2 + jnp.log2(total)
+    stat2_ref[1:2] = delta
+    stat2_ref[2:3] = shift * inverse
+    weights = weights * inverse
+    w_ref[...] = weights.astype(BF16)
+    ds_ref[...] = (weights * (prob_grad - delta)).astype(BF16)
+    dsib_ref[:, cols(0)] = (dot(ds_ref[...], q_ref[...], NN) * SCALING).astype(BF16)
+    dsib_ref[:, cols(1)] = dot(w_ref[...], g_ref[...], NN).astype(BF16)
 
 
 def mine_kernel(
-    own_ref, sib_ref, q_ref, g_ref, moved_ref, w_ref, ds_ref, down_ref, pair_ref
-):
-    dk, dv = key_terms(ds_ref[:HALF], w_ref[:HALF], q_ref, g_ref, moved_ref)
-    down_ref[:, cols(0)] = dk
-    down_ref[:, cols(1)] = dv
+    own_ref, sib_ref, q_ref, g_ref, e_ref, stat_ref, wsib_ref, dssib_ref,
+    down_ref, pair_ref, w_ref, ds_ref,
+):
+    prob_grad = dot(own_ref[:, cols(1)], g_ref[...], NT)
+    weights = e_ref[...] * stat_ref[2:3]
+    w_ref[...] = weights.astype(BF16)
+    ds_ref[...] = (weights * (prob_grad - stat_ref[1:2])).astype(BF16)
+    down_ref[:, cols(0)] = dot(ds_ref[...], q_ref[...], NN) * SCALING
+    down_ref[:, cols(1)] = dot(w_ref[...], g_ref[...], NN)
     results = []
-    for part, x_ref, factor in ((1, w_ref, 1.0), (0, ds_ref, SCALING)):
-        turned = dot(own_ref[:, cols(part)].T, x_ref[:HALF, head(GROUP)], NN)
-        turned += dot(sib_ref[:, cols(part)].T, x_ref[HALF:, head(GROUP)], NN)
+    for part, near_ref, far_ref, factor in (
+        (1, w_ref, wsib_ref, 1.0), (0, ds_ref, dssib_ref, SCALING)
+    ):
+        turned = dot(own_ref[:, cols(part)].T, near_ref[:, head(GROUP)], NN)
+        turned += dot(sib_ref[:, cols(part)].T, far_ref[:, head(GROUP)], NN)
         results.append((turned * factor).T)
     both = jnp.concatenate(results, axis=0).astype(BF16)
     pair_ref[...] = dot(deinterleave(1), both, NN).astype(BF16)
 
 
 def rest_kernel(
-    len_ref, aq_hbm, ak_hbm, av_hbm, ag_hbm, own_ref, sib_ref, w_ref, ds_ref, stat_ref,
-    aout_ref, adq_ref, adk_ref, adv_ref, q_ref, k_ref, v_ref, g_ref, sems,
+    len_ref, aq_hbm, ak_hbm, av_hbm, ag_hbm, own_ref, sib_ref,
+    w_ref, ds_ref, wsib_ref, dssib_ref, stat_ref,
+    aout_ref, adq_ref, adk_ref, adv_ref, q_ref, k_ref, v_ref, g_ref, out_ref, dq_ref, sems,
 ):
     pairs = ((aq_hbm, q_ref), (ak_hbm, k_ref), (av_hbm, v_ref), (ag_hbm, g_ref))
     copies = [pltpu.make_async_copy(a, b, sems.at[i]) for i, (a, b) in enumerate(pairs)]
     for copy in copies:
         copy.start()
-    for copy in copies:
-        copy.wait()
     length = len_ref[0]
     seen = seen_by(length)
     live_row = live_rows(length)
+    for part, near_ref, far_ref, sum_ref in (
+        (1, w_ref, wsib_ref, out_ref), (0, ds_ref, dssib_ref, dq_ref)
+    ):
+        sum_ref[...] = dot(own_ref[:, cols(part)].T, near_ref[:, :ROWS], NN)
+        sum_ref[...] += dot(sib_ref[:, cols(part)].T, far_ref[:, :ROWS], NN)
+    for copy in copies:
+        copy.wait()
     keys = k_ref[...]
     values = v_ref[...]
     keys_t = keys.T
     values_t = values.T
-    prompt_keys_t = jnp.concatenate([own_ref[:, cols(0)], sib_ref[:, cols(0)]], axis=0).T
-    prompt_values_t = jnp.concatenate([own_ref[:, cols(1)], sib_ref[:, cols(1)]], axis=0).T
     dk = jnp.zeros((ANS_LEN, HEAD_DIM), F32)
     dv = jnp.zeros((ANS_LEN, HEAD_DIM), F32)
     for n in range(GROUP):
@@ -315,12 +304,12 @@
         grads = g_ref[:, cols(n)]
         grads = jnp.where(live_row, grads, jnp.zeros_like(grads))
         scores = jnp.where(seen, dot(keys, queries, NT), NEG)
-        weights = jnp.exp2(scores * SCALE2 - stat_ref[n : n + 1])
+        weights = jnp.exp2(scores * SCALE2 - stat_ref[0:1, head(n)])
         weights_low = weights.astype(BF16)
-        product = dot(values, grads, NT) - stat_ref[8 + n : 9 + n]
+        product = dot(values, grads, NT) - stat_ref[1:2, head(n)]
         score_grad = (weights * product).astype(BF16)
-        out_t = dot(prompt_values_t, w_ref[:, head(n)], NN) + dot(values_t, weights_low, NN)
-        dq_t = dot(prompt_keys_t, ds_ref[:, head(n)], NN) + dot(keys_t, score_grad, NN)
+        out_t = out_ref[:, head(n)] + dot(values_t, weights_low, NN)
+        dq_t = dq_ref[:, head(n)] + dot(keys_t, score_grad, NN)
         aout_ref[:, cols(n)] = jnp.where(live_row, out_t.T, 0.0).astype(BF16)
         adq_ref[:, cols(n)] = (dq_t * SCALING).T.astype(BF16)
         dk += dot(score_grad, queries, NN)
@@ -389,7 +378,7 @@
     queries, grads, stat, bias = call(
         own_kernel,
         (
-            vmem(ROWS, HEAD_DIM), vmem(ROWS, HEAD_DIM), vmem(24, ANS_LEN, dtype=F32),
+            vmem(ROWS, HEAD_DIM), vmem(ROWS, HEAD_DIM), vmem(8, ROWS, dtype=F32),
             vmem(PROMPT, SENDERS, dtype=F32),
         ),
         [SMEM] + [HBM] * 5,
@@ -405,32 +394,35 @@
     )
     own, stat = lax.optimization_barrier((own, stat))
     sibling = lax.ppermute(own, "c", OTHER_CORE)
-    exps, bias, moved, stat, queries, grads = call(
+    exps, bias, stat, queries, grads = call(
         near_kernel,
         (
-            vmem(HALF, ALL, dtype=F32), vmem(HALF, SENDERS, dtype=F32), vmem(HALF, HEAD_DIM),
-            vmem(24, ANS_LEN, dtype=F32), vmem(ROWS, HEAD_DIM), vmem(ROWS, HEAD_DIM),
+            vmem(HALF, ALL, dtype=F32), vmem(HALF, SENDERS, dtype=F32),
+            vmem(8, ALL, dtype=F32), vmem(ALL, HEAD_DIM), vmem(ALL, HEAD_DIM),
         ),
         [VMEM] * 5,
         flops=200_000_000, moved=2_000_000,
     )(bias, own, queries, grads, stat)
-    d_sib, weights, score_grad, stat = call(
+    d_sib, far_w, far_ds, stat = call(
         far_kernel,
         (
-            vmem(HALF, 2 * HEAD_DIM), vmem(PROMPT, ALL), vmem(PROMPT, ALL),
-            vmem(16, ANS_LEN, dtype=F32),
+            vmem(HALF, 2 * HEAD_DIM), vmem(HALF, ALL), vmem(HALF, ALL),
+            vmem(8, ALL, dtype=F32),
+        ),
+        [VMEM] * 5,
+        flops=400_000_000, moved=2_000_000,
+    )(bias, sibling, queries, grads, stat)
+
+    d_mine = lax.ppermute(d_sib, "c", OTHER_CORE)
+    d_own, pair, near_w, near_ds = call(
+        mine_kernel,
+        (
+            vmem(HALF, 2 * HEAD_DIM, dtype=F32), vmem(HALF, HEAD_DIM),
+            vmem(HALF, ALL), vmem(HALF, ALL),
         ),
         [VMEM] * 8,
-        flops=400_000_000, moved=2_000_000,
-    )(bias, own, sibling, queries, grads, exps, moved, stat)
-
-    d_mine = lax.ppermute(d_sib, "c", OTHER_CORE)
-    d_own, pair = call(
-        mine_kernel,
-        (vmem(HALF, 2 * HEAD_DIM, dtype=F32), vmem(HALF, HEAD_DIM)),
-        [VMEM] * 7,
         flops=200_000_000, moved=2_000_000,
-    )(own, sibling, queries, grads, moved, weights, score_grad)
+    )(own, sibling, queries, grads, exps, stat, far_w, far_ds)
     back = call(
         post_kernel, bf16(SENDERS, 2, 3 * HEAD_DIM), [VMEM] * 3, limit=4, moved=700_000
     )(d_own, d_mine, pair)
@@ -442,16 +434,17 @@
             bf16(ANS_LEN, group), bf16(ANS_LEN, group),
             bf16(ANS_LEN, HEAD_DIM), bf16(ANS_LEN, HEAD_DIM),
         ),
-        [SMEM] + [HBM] * 4 + [VMEM] * 5,
+        [SMEM] + [HBM] * 4 + [VMEM] * 7,
         scratch=[
             pltpu.VMEM((ANS_LEN, group), BF16), pltpu.VMEM((ANS_LEN, HEAD_DIM), BF16),
             pltpu.VMEM((ANS_LEN, HEAD_DIM), BF16), pltpu.VMEM((ANS_LEN, group), BF16),
+            pltpu.VMEM((HEAD_DIM, ROWS), F32), pltpu.VMEM((HEAD_DIM, ROWS), F32),
             pltpu.SemaphoreType.DMA((4,)),
         ],
         flops=700_000_000, moved=2_000_000,
     )(
         answer_lengths, in_hbm(answer_q[0]), in_hbm(answer_k[0]), in_hbm(answer_v[0]),
-        in_hbm(answer_grad[0]), own, sibling, weights, score_grad, stat,
+        in_hbm(answer_grad[0]), own, sibling, near_w, near_ds, far_w, far_ds, stat,
     )
     p_out, p_dq, p_dk, p_dv = call(
         unpack_kernel, (bf16(2, wide), bf16(2, wide), bf16(2, narrow), bf16(2, narrow)), [VMEM],

time: 51.1 us -> 51.2 us (level)
  local copies, waits for them, and re-layouts: 0.75 us -> 0.07 us
    pallas_call x1, Pallas kernels: 0.11 us -> 0.79 us  [body(): call(post_kernel, bf16(SENDERS, 2, 3 * HEAD_DIM), [VMEM] * 3, limit=4, mo...]
    unnamed x2 -> x0, local copies, waits for them, and re-layouts: 0.67 us -> none
    all_to_all x2, waiting for transfers between devices: 2.02 us -> 2.6 us  [exchange(): lax.all_to_all(x, SEQ_AXES + HEAD_AXES, split_axis=0, concat_axis=0, tile...]
  transfers between devices with their start and end apart: 4 -> 4, of which waited for: 4 -> 3; matrix products, arithmetic and copies ran while one was open for 0% -> 0% of each run, Pallas kernels for 15% -> 15%
where the time goes in v4:
time: 51.2 us; the launch traced here: 50.8 us
  starting transfers between devices  34.2 us (67%)
  Pallas kernels  12.3 us (24%)
  waiting for transfers between devices  2.96 us (6%)
  between operations  1.35 us (3%)
    all_to_all x2, starting transfers between devices, exchange(): lax.all_to_all(x, SEQ_AXES + HEAD_AXES, split_axis=0, concat_axis=0, tile...  32.1 us
    pallas_call x1, Pallas kernels, body(): call(rest_kernel, (bf16(ANS_LEN, group), bf16(ANS_LEN, group), bf16(ANS_L...  3.89 us
    all_to_all x2, waiting for transfers between devices, exchange(): lax.all_to_all(x, SEQ_AXES + HEAD_AXES, split_axis=0, concat_axis=0, tile...  2.6 us
    pallas_call x1, Pallas kernels, body(): call(own_kernel, (vmem(ROWS, HEAD_DIM), vmem(ROWS, HEAD_DIM), vmem(8, ROW...  1.96 us
    ppermute x1, starting transfers between devices, body(): sibling = lax.ppermute(own, 'c', OTHER_CORE)  1.63 us
    pallas_call x1, Pallas kernels, body(): call(pack_kernel, bf16(SENDERS, 2, 3 * HEAD_DIM), [HBM] * 4, scratch=[plt...  1.6 us
    pallas_call x1, Pallas kernels, body(): call(far_kernel, (vmem(HALF, 2 * HEAD_DIM), vmem(HALF, ALL), vmem(HALF, A...  1.45 us
    pallas_call x1, Pallas kernels, body(): call(mine_kernel, (vmem(HALF, 2 * HEAD_DIM, dtype=F32), vmem(HALF, HEAD_D...  1.15 us
  transfers between devices with their start and end apart: 4, of which 3 were waited for; matrix products, arithmetic and copies ran while one was open for 0% of the time, Pallas kernels for 15%

profile of v4, /device:TPU:1, one launch (start us, length us, event | category | flops | bytes accessed | tf_op | source)
XLA Modules:
  0.0 50.8 jit_solution(1810701465427721230)
XLA Ops:
  0.6 1.6 %shard_map.161 = bf16[128,2,384]{2,1,0:T(2,128)(2,1)} custom-call(bf16[2,5120]{1,0:T(2,128)(2,1)} %q_hbm.1, bf16[2,5120]{1,0:T(2,128)(2,1)} %g_hbm.1, bf16[2,1024]{1,0:T(2,128)(2,1)} %k_hbm.1, bf16[2,1024]{1,0:T(2,128)(2,1)} %v_hbm.1), custom_call_target="tpu_custom_call" | custom-call | tf_op jit(solution)/shard_map/pallas_call | solution.py:363
  2.2 18.3 %all-to-all-start = ((bf16[128,2,384]{2,1,0:T(2,128)(2,1)}), bf16[128,2,384]{2,1,0:T(2,128)(2,1)S(1)}, u32[]{:S(2)}, u32[]{:S(2)}) async-start(bf16[128,2,384]{2,1,0:T(2,128)(2,1)} %shard_map.161), calls=%async_computation | async-start | bytes 393216 | tf_op jit(solution)/shard_map/all_to_all | solution.py:350
  21.2 2.0 %shard_map.162 = (bf16[1280,128]{1,0:T(8,128)(2,1)S(1)}, bf16[1280,128]{1,0:T(8,128)(2,1)S(1)}, f32[8,1280]{1,0:T(8,128)S(1)}, f32[512,128]{1,0:T(8,128)S(1)}) custom-call(s32[1]{0:T(128)S(6)} %copy.18.len_ref, s32[1,512]{1,0:T(1,128)} %bitcast.21, bf16[256,640]{1,0:T(8,128)(2,1)} %bitcast.9, bf16[256,128]{1,0:T(8,128)(2,1)} %bitcast.13, ...), custom_call_target="tpu_custom_call" | custom-call | flops 400000000 | bytes 2000000 | tf_op jit(solution)/shard_map/pallas_call | solution.py:378
  23.1 1.7 %all-to-all-done = bf16[128,2,384]{2,1,0:T(2,128)(2,1)S(1)} async-done(((bf16[128,2,384]{2,1,0:T(2,128)(2,1)}), bf16[128,2,384]{2,1,0:T(2,128)(2,1)S(1)}, u32[]{:S(2)}, u32[]{:S(2)}) %all-to-all-start) | async-done | bytes 196640 | tf_op jit(solution)/shard_map/all_to_all | solution.py:350
  24.9 0.1 reshape.22.own_ref
  24.9 1.6 %collective-permute-start = (bf16[256,384]{1,0:T(8,128)(2,1)S(1)}, bf16[256,384]{1,0:T(8,128)(2,1)S(1)}, u32[]{:S(2)}, u32[]{:S(2)}) collective-permute-start(bf16[256,384]{1,0:T(8,128)(2,1)S(1)} %reshape.22.own_ref), channel_id=1, source_target_pairs={{0,8},{8,0},{1,9},{9,1},{2,10},{10,2},{3,11},{11,3},{4,12},{12,4},... | collective-permute-start | bytes 589832 | tf_op jit(solution)/shard_map/ppermute | solution.py:396
  26.6 0.7 %shard_map.163 = (f32[256,1408]{1,0:T(8,128)S(1)}, f32[256,128]{1,0:T(8,128)S(1)}, f32[8,1408]{1,0:T(8,128)S(1)}, bf16[1408,128]{1,0:T(8,128)(2,1)S(1)}, bf16[1408,128]{1,0:T(8,128)(2,1)S(1)}) custom-call(f32[512,128]{1,0:T(8,128)S(1)} %get-tuple-element.43.bias_ref, bf16[256,384]{1,0:T(8,128)(2,1)S(1)} %reshape.22.own_ref, ...), custom_call_target="tpu_custom_call" | custom-call | flops 200000000 | bytes 2000000 | tf_op jit(solution)/shard_map/pallas_call | solution.py:397
  27.3 0.4 collective-permute-done.sib_ref
  27.6 1.5 %shard_map.164 = (bf16[256,256]{1,0:T(8,128)(2,1)S(1)}, bf16[256,1408]{1,0:T(8,128)(2,1)S(1)}, bf16[256,1408]{1,0:T(8,128)(2,1)S(1)}, f32[8,1408]{1,0:T(8,128)S(1)}) custom-call(f32[256,128]{1,0:T(8,128)S(1)} %get-tuple-element.50.bias_ref, bf16[256,384]{1,0:T(8,128)(2,1)S(1)} %collective-permute-done.sib_ref, ...), custom_call_target="tpu_custom_call" | custom-call | flops 400000000 | bytes 2000000 | tf_op jit(solution)/shard_map/pallas_call | solution.py:406
  29.1 0.5 collective-permute-start.1
  29.6 1.1 %shard_map.165 = (f32[256,256]{1,0:T(8,128)S(1)}, bf16[256,128]{1,0:T(8,128)(2,1)S(1)}, bf16[256,1408]{1,0:T(8,128)(2,1)S(1)}, bf16[256,1408]{1,0:T(8,128)(2,1)S(1)}) custom-call(bf16[256,384]{1,0:T(8,128)(2,1)S(1)} %reshape.22.own_ref, bf16[256,384]{1,0:T(8,128)(2,1)S(1)} %collective-permute-done.sib_ref, bf16[1408,128]{1,0:T(8,128)(2,1)S(1)} %get-tuple-element.47.q_ref, ...), custom_call_target="tpu_custom_call" | custom-call | flops 200000000 | bytes 2000000 | tf_op jit(solution)/shard_map/pallas_call | solution.py:417
  30.7 0.0 collective-permute-done.1.other_ref
  30.7 0.8 %shard_map.166 = bf16[128,2,384]{2,1,0:T(2,128)(2,1)} custom-call(f32[256,256]{1,0:T(8,128)S(1)} %get-tuple-element.55.own_ref, bf16[256,256]{1,0:T(8,128)(2,1)S(1)} %collective-permute-done.1.other_ref, bf16[256,128]{1,0:T(8,128)(2,1)S(1)} %get-tuple-element.57.pair_ref), custom_call_target="tpu_custom_call" | custom-call | bytes 700000 | tf_op jit(solution)/shard_map/pallas_call | solution.py:426
  31.5 13.8 %all-to-all-start.1 = ((bf16[128,2,384]{2,1,0:T(2,128)(2,1)}), bf16[128,2,384]{2,1,0:T(2,128)(2,1)S(1)}, u32[]{:S(2)}, u32[]{:S(2)}) async-start(bf16[128,2,384]{2,1,0:T(2,128)(2,1)} %shard_map.166), calls=%async_computation.1 | async-start | bytes 393216 | tf_op jit(solution)/shard_map/all_to_all | solution.py:350
  45.3 3.9 %shard_map.168 = (bf16[256,640]{1,0:T(8,128)(2,1)}, bf16[256,640]{1,0:T(8,128)(2,1)}, bf16[256,128]{1,0:T(8,128)(2,1)}, bf16[256,128]{1,0:T(8,128)(2,1)}) custom-call(s32[1]{0:T(128)S(6)} %copy.18.len_ref, bf16[256,640]{1,0:T(8,128)(2,1)} %bitcast.10, bf16[256,128]{1,0:T(8,128)(2,1)} %bitcast.14, bf16[256,128]{1,0:T(8,128)(2,1)} %bitcast.16, ...), custom_call_target="tpu_custom_call" | custom-call | flops 700000000 | bytes 2000000 | tf_op jit(solution)/shard_map/pallas_call | solution.py:431
  49.2 0.9 %all-to-all-done.1.x_ref = bf16[128,2,384]{2,1,0:T(2,128)(2,1)S(1)} async-done(((bf16[128,2,384]{2,1,0:T(2,128)(2,1)}), bf16[128,2,384]{2,1,0:T(2,128)(2,1)S(1)}, u32[]{:S(2)}, u32[]{:S(2)}) %all-to-all-start.1) | async-done | bytes 196640 | tf_op jit(solution)/shard_map/all_to_all | solution.py:350
  50.1 0.7 %shard_map.167 = (bf16[2,5120]{1,0:T(2,128)(2,1)}, bf16[2,5120]{1,0:T(2,128)(2,1)}, bf16[2,1024]{1,0:T(2,128)(2,1)}, bf16[2,1024]{1,0:T(2,128)(2,1)}) custom-call(bf16[128,2,384]{2,1,0:T(2,128)(2,1)S(1)} %all-to-all-done.1.x_ref), custom_call_target="tpu_custom_call" | custom-call | tf_op jit(solution)/shard_map/pallas_call | solution.py:449
Async XLA Ops:
  2.2 22.6 %all-to-all-start = ((bf16[128,2,384]{2,1,0:T(2,128)(2,1)}), bf16[128,2,384]{2,1,0:T(2,128)(2,1)S(1)}, u32[]{:S(2)}, u32[]{:S(2)}) async-start(bf16[128,2,384]{2,1,0:T(2,128)(2,1)} %shard_map.161), calls=%async_computation | async-start | bytes 393216 | tf_op jit(solution)/shard_map/all_to_all | solution.py:350
  24.9 2.7 %collective-permute-start = (bf16[256,384]{1,0:T(8,128)(2,1)S(1)}, bf16[256,384]{1,0:T(8,128)(2,1)S(1)}, u32[]{:S(2)}, u32[]{:S(2)}) collective-permute-start(bf16[256,384]{1,0:T(8,128)(2,1)S(1)} %reshape.22.own_ref), channel_id=1, source_target_pairs={{0,8},{8,0},{1,9},{9,1},{2,10},{10,2},{3,11},{11,3},{4,12},{12,4},... | collective-permute-start | bytes 589832 | tf_op jit(solution)/shard_map/ppermute | solution.py:396
  29.1 1.6 %collective-permute-start.1 = (bf16[256,256]{1,0:T(8,128)(2,1)S(1)}, bf16[256,256]{1,0:T(8,128)(2,1)S(1)}, u32[]{:S(2)}, u32[]{:S(2)}) collective-permute-start(bf16[256,256]{1,0:T(8,128)(2,1)S(1)} %get-tuple-element.56), channel_id=1, source_target_pairs={{0,8},{8,0},{1,9},{9,1},{2,10},{10,2},{3,11},{11,3},{4,12},{12,4},... | collective-permute-start | bytes 393224 | tf_op jit(solution)/shard_map/ppermute | solution.py:416
  31.5 18.6 %all-to-all-start.1 = ((bf16[128,2,384]{2,1,0:T(2,128)(2,1)}), bf16[128,2,384]{2,1,0:T(2,128)(2,1)S(1)}, u32[]{:S(2)}, u32[]{:S(2)}) async-start(bf16[128,2,384]{2,1,0:T(2,128)(2,1)} %shard_map.166), calls=%async_computation.1 | async-start | bytes 393216 | tf_op jit(solution)/shard_map/all_to_all | solution.py:350

commit v5 on v4

--- a/solution.py
+++ b/solution.py
@@ -80,7 +80,13 @@
     copies = [pltpu.make_async_copy(a, b, sems.at[i]) for i, (a, b) in enumerate(pairs)]
     for copy in copies:
         copy.start()
-    for copy in copies:
+    for copy in copies[:2]:
+        copy.wait()
+    for peer in range(SENDERS):
+        h = group_of(peer)
+        o_ref[peer, :, cols(0)] = k_ref[:, cols(h)]
+        o_ref[peer, :, cols(1)] = v_ref[:, cols(h)]
+    for copy in copies[2:]:
         copy.wait()
     q = q_ref[...].astype(F32)
     g = g_ref[...].astype(F32)
@@ -89,8 +95,6 @@
     for peer in range(SENDERS):
         h = group_of(peer)
         d = place_of(peer)
-        o_ref[peer, :, cols(0)] = k_ref[:, cols(h)]
-        o_ref[peer, :, cols(1)] = v_ref[:, cols(h)]
         if d < PAIRS:
             pair = rows[d // GROUP][:, cols(h * GROUP + d % GROUP)]
         else:

time: 51.2 us -> 51.1 us (level)
  no operation moved by 1% of the time
where the time goes in v5:
time: 51.1 us; the launch traced here: 50.7 us
  starting transfers between devices  34.1 us (67%)
  Pallas kernels  12.2 us (24%)
  waiting for transfers between devices  2.96 us (6%)
  between operations  1.35 us (3%)
    all_to_all x2, starting transfers between devices, exchange(): lax.all_to_all(x, SEQ_AXES + HEAD_AXES, split_axis=0, concat_axis=0, tile...  32.1 us
    pallas_call x1, Pallas kernels, body(): call(rest_kernel, (bf16(ANS_LEN, group), bf16(ANS_LEN, group), bf16(ANS_L...  3.89 us
    all_to_all x2, waiting for transfers between devices, exchange(): lax.all_to_all(x, SEQ_AXES + HEAD_AXES, split_axis=0, concat_axis=0, tile...  2.6 us
    pallas_call x1, Pallas kernels, body(): call(own_kernel, (vmem(ROWS, HEAD_DIM), vmem(ROWS, HEAD_DIM), vmem(8, ROW...  1.96 us
    ppermute x1, starting transfers between devices, body(): sibling = lax.ppermute(own, 'c', OTHER_CORE)  1.63 us
    pallas_call x1, Pallas kernels, body(): call(pack_kernel, bf16(SENDERS, 2, 3 * HEAD_DIM), [HBM] * 4, scratch=[plt...  1.54 us
    pallas_call x1, Pallas kernels, body(): call(far_kernel, (vmem(HALF, 2 * HEAD_DIM), vmem(HALF, ALL), vmem(HALF, A...  1.45 us
    pallas_call x1, Pallas kernels, body(): call(mine_kernel, (vmem(HALF, 2 * HEAD_DIM, dtype=F32), vmem(HALF, HEAD_D...  1.15 us
  transfers between devices with their start and end apart: 4, of which 3 were waited for; matrix products, arithmetic and copies ran while one was open for 0% of the time, Pallas kernels for 15%

profile of v5, /device:TPU:1, one launch (start us, length us, event | category | flops | bytes accessed | tf_op | source)
XLA Modules:
  0.0 50.7 jit_solution(17744894694013017789)
XLA Ops:
  0.6 1.5 %shard_map.161 = bf16[128,2,384]{2,1,0:T(2,128)(2,1)} custom-call(bf16[2,5120]{1,0:T(2,128)(2,1)} %q_hbm.1, bf16[2,5120]{1,0:T(2,128)(2,1)} %g_hbm.1, bf16[2,1024]{1,0:T(2,128)(2,1)} %k_hbm.1, bf16[2,1024]{1,0:T(2,128)(2,1)} %v_hbm.1), custom_call_target="tpu_custom_call" | custom-call | tf_op jit(solution)/shard_map/pallas_call | solution.py:367
  2.2 18.3 %all-to-all-start = ((bf16[128,2,384]{2,1,0:T(2,128)(2,1)}), bf16[128,2,384]{2,1,0:T(2,128)(2,1)S(1)}, u32[]{:S(2)}, u32[]{:S(2)}) async-start(bf16[128,2,384]{2,1,0:T(2,128)(2,1)} %shard_map.161), calls=%async_computation | async-start | bytes 393216 | tf_op jit(solution)/shard_map/all_to_all | solution.py:354
  21.1 2.0 %shard_map.162 = (bf16[1280,128]{1,0:T(8,128)(2,1)S(1)}, bf16[1280,128]{1,0:T(8,128)(2,1)S(1)}, f32[8,1280]{1,0:T(8,128)S(1)}, f32[512,128]{1,0:T(8,128)S(1)}) custom-call(s32[1]{0:T(128)S(6)} %copy.18.len_ref, s32[1,512]{1,0:T(1,128)} %bitcast.21, bf16[256,640]{1,0:T(8,128)(2,1)} %bitcast.9, bf16[256,128]{1,0:T(8,128)(2,1)} %bitcast.13, ...), custom_call_target="tpu_custom_call" | custom-call | flops 400000000 | bytes 2000000 | tf_op jit(solution)/shard_map/pallas_call | solution.py:382
  23.1 1.7 %all-to-all-done = bf16[128,2,384]{2,1,0:T(2,128)(2,1)S(1)} async-done(((bf16[128,2,384]{2,1,0:T(2,128)(2,1)}), bf16[128,2,384]{2,1,0:T(2,128)(2,1)S(1)}, u32[]{:S(2)}, u32[]{:S(2)}) %all-to-all-start) | async-done | bytes 196640 | tf_op jit(solution)/shard_map/all_to_all | solution.py:354
  24.8 0.1 reshape.22.own_ref
  24.9 1.6 %collective-permute-start = (bf16[256,384]{1,0:T(8,128)(2,1)S(1)}, bf16[256,384]{1,0:T(8,128)(2,1)S(1)}, u32[]{:S(2)}, u32[]{:S(2)}) collective-permute-start(bf16[256,384]{1,0:T(8,128)(2,1)S(1)} %reshape.22.own_ref), channel_id=1, source_target_pairs={{0,8},{8,0},{1,9},{9,1},{2,10},{10,2},{3,11},{11,3},{4,12},{12,4},... | collective-permute-start | bytes 589832 | tf_op jit(solution)/shard_map/ppermute | solution.py:400
  26.5 0.7 %shard_map.163 = (f32[256,1408]{1,0:T(8,128)S(1)}, f32[256,128]{1,0:T(8,128)S(1)}, f32[8,1408]{1,0:T(8,128)S(1)}, bf16[1408,128]{1,0:T(8,128)(2,1)S(1)}, bf16[1408,128]{1,0:T(8,128)(2,1)S(1)}) custom-call(f32[512,128]{1,0:T(8,128)S(1)} %get-tuple-element.43.bias_ref, bf16[256,384]{1,0:T(8,128)(2,1)S(1)} %reshape.22.own_ref, ...), custom_call_target="tpu_custom_call" | custom-call | flops 200000000 | bytes 2000000 | tf_op jit(solution)/shard_map/pallas_call | solution.py:401
  27.2 0.4 collective-permute-done.sib_ref
  27.6 1.5 %shard_map.164 = (bf16[256,256]{1,0:T(8,128)(2,1)S(1)}, bf16[256,1408]{1,0:T(8,128)(2,1)S(1)}, bf16[256,1408]{1,0:T(8,128)(2,1)S(1)}, f32[8,1408]{1,0:T(8,128)S(1)}) custom-call(f32[256,128]{1,0:T(8,128)S(1)} %get-tuple-element.50.bias_ref, bf16[256,384]{1,0:T(8,128)(2,1)S(1)} %collective-permute-done.sib_ref, ...), custom_call_target="tpu_custom_call" | custom-call | flops 400000000 | bytes 2000000 | tf_op jit(solution)/shard_map/pallas_call | solution.py:410
  29.0 0.5 collective-permute-start.1
  29.5 1.1 %shard_map.165 = (f32[256,256]{1,0:T(8,128)S(1)}, bf16[256,128]{1,0:T(8,128)(2,1)S(1)}, bf16[256,1408]{1,0:T(8,128)(2,1)S(1)}, bf16[256,1408]{1,0:T(8,128)(2,1)S(1)}) custom-call(bf16[256,384]{1,0:T(8,128)(2,1)S(1)} %reshape.22.own_ref, bf16[256,384]{1,0:T(8,128)(2,1)S(1)} %collective-permute-done.sib_ref, bf16[1408,128]{1,0:T(8,128)(2,1)S(1)} %get-tuple-element.47.q_ref, ...), custom_call_target="tpu_custom_call" | custom-call | flops 200000000 | bytes 2000000 | tf_op jit(solution)/shard_map/pallas_call | solution.py:421
  30.7 0.0 collective-permute-done.1.other_ref
  30.7 0.8 %shard_map.166 = bf16[128,2,384]{2,1,0:T(2,128)(2,1)} custom-call(f32[256,256]{1,0:T(8,128)S(1)} %get-tuple-element.55.own_ref, bf16[256,256]{1,0:T(8,128)(2,1)S(1)} %collective-permute-done.1.other_ref, bf16[256,128]{1,0:T(8,128)(2,1)S(1)} %get-tuple-element.57.pair_ref), custom_call_target="tpu_custom_call" | custom-call | bytes 700000 | tf_op jit(solution)/shard_map/pallas_call | solution.py:430
  31.5 13.8 %all-to-all-start.1 = ((bf16[128,2,384]{2,1,0:T(2,128)(2,1)}), bf16[128,2,384]{2,1,0:T(2,128)(2,1)S(1)}, u32[]{:S(2)}, u32[]{:S(2)}) async-start(bf16[128,2,384]{2,1,0:T(2,128)(2,1)} %shard_map.166), calls=%async_computation.1 | async-start | bytes 393216 | tf_op jit(solution)/shard_map/all_to_all | solution.py:354
  45.2 3.9 %shard_map.168 = (bf16[256,640]{1,0:T(8,128)(2,1)}, bf16[256,640]{1,0:T(8,128)(2,1)}, bf16[256,128]{1,0:T(8,128)(2,1)}, bf16[256,128]{1,0:T(8,128)(2,1)}) custom-call(s32[1]{0:T(128)S(6)} %copy.18.len_ref, bf16[256,640]{1,0:T(8,128)(2,1)} %bitcast.10, bf16[256,128]{1,0:T(8,128)(2,1)} %bitcast.14, bf16[256,128]{1,0:T(8,128)(2,1)} %bitcast.16, ...), custom_call_target="tpu_custom_call" | custom-call | flops 700000000 | bytes 2000000 | tf_op jit(solution)/shard_map/pallas_call | solution.py:435
  49.1 0.9 %all-to-all-done.1.x_ref = bf16[128,2,384]{2,1,0:T(2,128)(2,1)S(1)} async-done(((bf16[128,2,384]{2,1,0:T(2,128)(2,1)}), bf16[128,2,384]{2,1,0:T(2,128)(2,1)S(1)}, u32[]{:S(2)}, u32[]{:S(2)}) %all-to-all-start.1) | async-done | bytes 196640 | tf_op jit(solution)/shard_map/all_to_all | solution.py:354
  50.0 0.7 %shard_map.167 = (bf16[2,5120]{1,0:T(2,128)(2,1)}, bf16[2,5120]{1,0:T(2,128)(2,1)}, bf16[2,1024]{1,0:T(2,128)(2,1)}, bf16[2,1024]{1,0:T(2,128)(2,1)}) custom-call(bf16[128,2,384]{2,1,0:T(2,128)(2,1)S(1)} %all-to-all-done.1.x_ref), custom_call_target="tpu_custom_call" | custom-call | tf_op jit(solution)/shard_map/pallas_call | solution.py:453
Async XLA Ops:
  2.2 22.6 %all-to-all-start = ((bf16[128,2,384]{2,1,0:T(2,128)(2,1)}), bf16[128,2,384]{2,1,0:T(2,128)(2,1)S(1)}, u32[]{:S(2)}, u32[]{:S(2)}) async-start(bf16[128,2,384]{2,1,0:T(2,128)(2,1)} %shard_map.161), calls=%async_computation | async-start | bytes 393216 | tf_op jit(solution)/shard_map/all_to_all | solution.py:354
  24.9 2.7 %collective-permute-start = (bf16[256,384]{1,0:T(8,128)(2,1)S(1)}, bf16[256,384]{1,0:T(8,128)(2,1)S(1)}, u32[]{:S(2)}, u32[]{:S(2)}) collective-permute-start(bf16[256,384]{1,0:T(8,128)(2,1)S(1)} %reshape.22.own_ref), channel_id=1, source_target_pairs={{0,8},{8,0},{1,9},{9,1},{2,10},{10,2},{3,11},{11,3},{4,12},{12,4},... | collective-permute-start | bytes 589832 | tf_op jit(solution)/shard_map/ppermute | solution.py:400
  29.0 1.6 %collective-permute-start.1 = (bf16[256,256]{1,0:T(8,128)(2,1)S(1)}, bf16[256,256]{1,0:T(8,128)(2,1)S(1)}, u32[]{:S(2)}, u32[]{:S(2)}) collective-permute-start(bf16[256,256]{1,0:T(8,128)(2,1)S(1)} %get-tuple-element.56), channel_id=1, source_target_pairs={{0,8},{8,0},{1,9},{9,1},{2,10},{10,2},{3,11},{11,3},{4,12},{12,4},... | collective-permute-start | bytes 393224 | tf_op jit(solution)/shard_map/ppermute | solution.py:420
  31.5 18.6 %all-to-all-start.1 = ((bf16[128,2,384]{2,1,0:T(2,128)(2,1)}), bf16[128,2,384]{2,1,0:T(2,128)(2,1)S(1)}, u32[]{:S(2)}, u32[]{:S(2)}) async-start(bf16[128,2,384]{2,1,0:T(2,128)(2,1)} %shard_map.166), calls=%async_computation.1 | async-start | bytes 393216 | tf_op jit(solution)/shard_map/all_to_all | solution.py:354
